TPU v7x, 32 devices: a whole 2x2x4 slice. The times are simulated.
32 devices in a mesh: dp: 8 (over z, y), tensor: 4 (over x, core).
Axes of the slice: x: 2, y: 2, z: 4, core: 2. Of those that a mesh axis runs over, the one named last changes fastest.
Arguments:
- tokens: bfloat16 [8192, 512], P('dp'), may hold values from -6 to 6
- memory: bfloat16 [8192, 512], P('dp'), may hold values from -6 to 6
- cotangent: bfloat16 [8192, 512], P('dp'), may hold values from -6 to 6
- lengths: int32 [16], P('dp'), may hold values from 1 to 512, 6144 in all
- breaks: int32 [16], P('dp'), may hold values from 1 to 501
- attn_in: float32 [6, 512, 512], P(None, 'dp', 'tensor'), may hold values from -0.25 to 0.25
- attn_out: float32 [2, 512, 512], P(None, 'dp', 'tensor'), may hold values from -3 to 3
- ffn_in: float32 [512, 2048], P('dp', 'tensor'), may hold values from -0.25 to 0.25
- ffn_out: float32 [512, 2048], P('dp', 'tensor'), may hold values from -0.125 to 0.125
- norms: float32 [6, 512], P(None, 'dp'), may hold values from -0.9 to 1.3, as said below
- attn_in_mom: float32 [6, 512, 512], P(None, 'dp', 'tensor'), may hold values from -256 to 256
- attn_out_mom: float32 [2, 512, 512], P(None, 'dp', 'tensor'), may hold values from -64 to 64
- ffn_in_mom: float32 [512, 2048], P('dp', 'tensor'), may hold values from -256 to 256
- ffn_out_mom: float32 [512, 2048], P('dp', 'tensor'), may hold values from -256 to 256
- norms_mom: float32 [6, 512], P(None, 'dp'), may hold values from -256 to 256
- attn_in_avg: float32 [6, 512, 512], P(None, 'dp', 'tensor'), may hold values from -0.25 to 0.25
- attn_out_avg: float32 [2, 512, 512], P(None, 'dp', 'tensor'), may hold values from -3 to 3
- ffn_in_avg: float32 [512, 2048], P('dp', 'tensor'), may hold values from -0.25 to 0.25
- ffn_out_avg: float32 [512, 2048], P('dp', 'tensor'), may hold values from -0.125 to 0.125
- norms_avg: float32 [6, 512], P(None, 'dp'), may hold values from 0.5 to 1.5
Outputs:
- block_out: bfloat16 [8192, 512], P('dp')
- tokens_grad: float32 [8192, 512], P('dp')
- attn_in_grad: float32 [6, 512, 512], P(None, 'dp', 'tensor')
- attn_in_mom_new: float32 [6, 512, 512], P(None, 'dp', 'tensor')
- attn_in_new: float32 [6, 512, 512], P(None, 'dp', 'tensor')
- attn_in_avg_new: float32 [6, 512, 512], P(None, 'dp', 'tensor')
- attn_out_grad: float32 [2, 512, 512], P(None, 'dp', 'tensor')
- attn_out_mom_new: float32 [2, 512, 512], P(None, 'dp', 'tensor')
- attn_out_new: float32 [2, 512, 512], P(None, 'dp', 'tensor')
- attn_out_avg_new: float32 [2, 512, 512], P(None, 'dp', 'tensor')
- ffn_in_grad: float32 [512, 2048], P('dp', 'tensor')
- ffn_in_mom_new: float32 [512, 2048], P('dp', 'tensor')
- ffn_in_new: float32 [512, 2048], P('dp', 'tensor')
- ffn_in_avg_new: float32 [512, 2048], P('dp', 'tensor')
- ffn_out_grad: float32 [512, 2048], P('dp', 'tensor')
- ffn_out_mom_new: float32 [512, 2048], P('dp', 'tensor')
- ffn_out_new: float32 [512, 2048], P('dp', 'tensor')
- ffn_out_avg_new: float32 [512, 2048], P('dp', 'tensor')
- norms_grad: float32 [6, 512], P(None, 'dp')
- norms_mom_new: float32 [6, 512], P(None, 'dp')
- norms_new: float32 [6, 512], P(None, 'dp')
- norms_avg_new: float32 [6, 512], P(None, 'dp')
Inputs may be any that keep to these rules, and one draw needn't show every extreme that they name: Positions at and beyond a protein's length are padding; the largest length is 512 in every draw, and the lengths sum to 6144. The linker slots breaks to breaks + 9 are padding between the first and the second chain; where they lie at or beyond the length the complex holds one chain. `norms`: rows 0, 2, 4 are gains, rows 1, 3, 5 biases.
All inputs are finite; a program needn't handle non-finite values. No bound on the sum of `lengths` on one device may be relied on, other than what follows from the above.
Results may differ from a plain program's by a relative error of at most 0.02.
The roundings to bfloat16 on the way count: a program that leaves them out, or rounds other values in their place, can miss the bound.
Values may be sent and summed in bfloat16 or wider, within the bound.
A program may use at most 128 MiB of HBM per device.

v0:
```python
from functools import partial

import jax
import jax.numpy as jnp
from jax import lax
from jax.sharding import PartitionSpec as P

HD = 64
SEQ = 512
LINKER = 10


EPSILON = 1e-05
NEG_FILL = -1000000000.0
MOMENTUM = 0.9
AVG_DECAY = 0.6
BASE_RATES = (0.05, 1.0, 0.05, 0.05, 0.3)


def layer_norm(values, gain_row, bias_row):
    center = values - jnp.mean(values, -1, keepdims=True)
    spread = jnp.mean(center * center, -1, keepdims=True)
    inv_std = lax.rsqrt(spread + EPSILON)
    x_hat = center * inv_std
    return (x_hat * gain_row + bias_row, x_hat, inv_std)


def norm_back(grad_h, x_hat, inv_std, gain_row):
    grad_gain = jnp.sum(grad_h * x_hat, 0)
    grad_bias = jnp.sum(grad_h, 0)
    grad_hat = grad_h * gain_row
    grad_in = inv_std * (
        grad_hat
        - jnp.mean(grad_hat, -1, keepdims=True)
        - x_hat * jnp.mean(grad_hat * x_hat, -1, keepdims=True)
    )
    return (grad_in, grad_gain, grad_bias)


def matmul_in(left_op, right_op):
    return jnp.dot(left_op, right_op, preferred_element_type=jnp.float32)


def matmul_tr(left_op, right_op):
    return lax.dot_general(
        left_op, right_op, (((1,), (1,)), ((), ())), preferred_element_type=jnp.float32
    )


def weight_grad(left_op, right_op):
    return lax.dot_general(
        left_op, right_op, (((0,), (0,)), ((), ())), preferred_element_type=jnp.float32
    )


def score_block(query, keys_b, mask_ok):
    seq_len = query.shape[0]
    query_h = query.reshape(seq_len, -1, HD)
    keys_h = keys_b.reshape(keys_b.shape[0], -1, HD)
    scores = jnp.einsum(
        "qhe,khe->hqk", query_h, keys_h, preferred_element_type=jnp.float32
    ) * HD ** (-0.5)
    return jnp.where(mask_ok[None], scores, NEG_FILL)


def attend_fwd(query, keys_b, values_b, mask_ok):
    seq_len = query.shape[0]
    scores = score_block(query, keys_b, mask_ok)
    top_score = jnp.max(scores, -1, keepdims=True)
    log_total = top_score + jnp.log(jnp.sum(jnp.exp(scores - top_score), -1, keepdims=True))
    prob_low = jnp.exp(scores - log_total).astype(jnp.bfloat16)
    values_h = values_b.reshape(values_b.shape[0], -1, HD)
    mixed = jnp.einsum("hqk,khe->qhe", prob_low, values_h, preferred_element_type=jnp.float32)
    return (mixed.reshape(seq_len, -1).astype(jnp.bfloat16), log_total)


def attend_back(grad_low, query, keys_b, values_b, log_total, mask_ok):
    seq_len = query.shape[0]
    scale_val = HD ** (-0.5)
    query_h = query.reshape(seq_len, -1, HD)
    keys_h = keys_b.reshape(keys_b.shape[0], -1, HD)
    values_h = values_b.reshape(values_b.shape[0], -1, HD)
    grad_h = grad_low.reshape(seq_len, -1, HD)
    attn_prob = jnp.exp(score_block(query, keys_b, mask_ok) - log_total)
    prob_low = attn_prob.astype(jnp.bfloat16)
    grad_prob = jnp.einsum("qhe,khe->hqk", grad_h, values_h, preferred_element_type=jnp.float32)
    inner_sum = jnp.sum(attn_prob * grad_prob, -1, keepdims=True)
    grad_score = (attn_prob * (grad_prob - inner_sum)).astype(jnp.bfloat16)
    grad_query = (
        jnp.einsum("hqk,khe->qhe", grad_score, keys_h, preferred_element_type=jnp.float32)
        * scale_val
    )
    grad_keys = (
        jnp.einsum("hqk,qhe->khe", grad_score, query_h, preferred_element_type=jnp.float32)
        * scale_val
    )
    grad_values = jnp.einsum("hqk,qhe->khe", prob_low, grad_h, preferred_element_type=jnp.float32)
    return (
        grad_query.reshape(seq_len, -1).astype(jnp.bfloat16),
        grad_keys.reshape(keys_b.shape[0], -1).astype(jnp.bfloat16),
        grad_values.reshape(values_b.shape[0], -1).astype(jnp.bfloat16),
    )


def update(weight, grad_sum, moment, average, rate):
    moment_new = MOMENTUM * moment + grad_sum
    weight_new = weight - rate * (grad_sum + MOMENTUM * moment_new)
    average_new = AVG_DECAY * average + (1.0 - AVG_DECAY) * weight_new
    return (grad_sum, moment_new, weight_new, average_new)


def per_device(
    tokens,
    memory,
    cotangent,
    lengths,
    breaks,
    attn_in,
    attn_out,
    ffn_in,
    ffn_out,
    norms,
    attn_in_mom,
    attn_out_mom,
    ffn_in_mom,
    ffn_out_mom,
    norms_mom,
    attn_in_avg,
    attn_out_avg,
    ffn_in_avg,
    ffn_out_avg,
    norms_avg,
):
    low_type = jnp.bfloat16
    in_rows, out_rows, norm_rows = (
        lax.all_gather(attn_in.astype(low_type), "dp", axis=1, tiled=True),
        lax.all_gather(attn_out.astype(low_type), "dp", axis=1, tiled=True),
        lax.all_gather(norms.astype(low_type), "dp", axis=1, tiled=True),
    )
    up_rows, down_rows = (
        lax.all_gather(ffn_in.astype(low_type), "dp", axis=0, tiled=True),
        lax.all_gather(ffn_out.astype(low_type), "dp", axis=0, tiled=True),
    )
    gain_all = norm_rows.astype(jnp.float32)
    gelu_fn = partial(jax.nn.gelu, approximate=False)

    def add_branch(resid, part_out):
        return resid + lax.psum(part_out, "tensor")

    def sum_grad(part_grad):
        return lax.psum(part_grad, "tensor")

    def protein_step(totals, item):
        tok_b, mem_b, cot_b, length_n, break_n = item
        tokens_f = tok_b.astype(jnp.float32)
        positions = jnp.arange(SEQ)
        linker = (positions >= break_n) & (positions < break_n + LINKER)
        live = (positions < length_n) & jnp.logical_not(linker)
        key_live = live[None, :]
        self_ok = (positions[None, :] <= positions[:, None]) & key_live
        cross_ok = jnp.broadcast_to(key_live, (SEQ, SEQ))
        h_one, hat_one, inv_one = layer_norm(tokens_f, gain_all[0], gain_all[1])
        h_one_b = h_one.astype(low_type)
        q_self = matmul_in(h_one_b, in_rows[0]).astype(low_type)
        k_self = matmul_in(h_one_b, in_rows[1]).astype(low_type)
        v_self = matmul_in(h_one_b, in_rows[2]).astype(low_type)
        a_self, lse_self = attend_fwd(q_self, k_self, v_self, self_ok)
        x_one = add_branch(tokens_f, matmul_tr(a_self, out_rows[0]))
        h_two, hat_two, inv_two = layer_norm(x_one, gain_all[2], gain_all[3])
        h_two_b = h_two.astype(low_type)
        q_cross = matmul_in(h_two_b, in_rows[3]).astype(low_type)
        k_cross = matmul_in(mem_b, in_rows[4]).astype(low_type)
        v_cross = matmul_in(mem_b, in_rows[5]).astype(low_type)
        a_cross, lse_cross = attend_fwd(q_cross, k_cross, v_cross, cross_ok)
        x_two = add_branch(x_one, matmul_tr(a_cross, out_rows[1]))
        h_three, hat_three, inv_three = layer_norm(x_two, gain_all[4], gain_all[5])
        h_three_b = h_three.astype(low_type)
        hidden = matmul_in(h_three_b, up_rows)
        act_low = gelu_fn(hidden).astype(low_type)
        out_part = add_branch(x_two, matmul_tr(act_low, down_rows))
        block_out = out_part.astype(low_type)
        row_live = live.astype(jnp.float32)[:, None]
        grad_out = cot_b.astype(jnp.float32) * row_live
        grad_z = grad_out.astype(low_type)
        grad_down = weight_grad(grad_z, act_low)
        grad_act = matmul_in(grad_z, down_rows)
        gelu_out, gelu_pull = jax.vjp(gelu_fn, hidden)
        grad_hidden = gelu_pull(grad_act)[0].astype(low_type)
        grad_up = weight_grad(h_three_b, grad_hidden)
        dh_three = sum_grad(matmul_tr(grad_hidden, up_rows))
        dx_norm3, gain_g3, bias_g3 = norm_back(dh_three, hat_three, inv_three, gain_all[4])
        dx_two = grad_out + dx_norm3
        dy_cross = dx_two.astype(low_type)
        grad_o_cross = weight_grad(dy_cross, a_cross)
        do_cross = matmul_in(dy_cross, out_rows[1]).astype(low_type)
        dq_cross, dk_cross, dv_cross = attend_back(
            do_cross, q_cross, k_cross, v_cross, lse_cross, cross_ok
        )
        grad_q_cross = weight_grad(h_two_b, dq_cross)
        grad_k_cross = weight_grad(mem_b, dk_cross)
        grad_v_cross = weight_grad(mem_b, dv_cross)
        dh_two = sum_grad(matmul_tr(dq_cross, in_rows[3]))
        dx_norm2, gain_g2, bias_g2 = norm_back(dh_two, hat_two, inv_two, gain_all[2])
        dx_one = dx_two + dx_norm2
        dy_self = dx_one.astype(low_type)
        grad_o_self = weight_grad(dy_self, a_self)
        do_self = matmul_in(dy_self, out_rows[0]).astype(low_type)
        dq_self, dk_self, dv_self = attend_back(do_self, q_self, k_self, v_self, lse_self, self_ok)
        grad_q_self = weight_grad(h_one_b, dq_self)
        grad_k_self = weight_grad(h_one_b, dk_self)
        grad_v_self = weight_grad(h_one_b, dv_self)
        dh_one = sum_grad(
            matmul_tr(dq_self, in_rows[0])
            + matmul_tr(dk_self, in_rows[1])
            + matmul_tr(dv_self, in_rows[2])
        )
        dx_norm1, gain_g1, bias_g1 = norm_back(dh_one, hat_one, inv_one, gain_all[0])
        tokens_grad = dx_one + dx_norm1
        grad_in_all = jnp.stack(
            [grad_q_self, grad_k_self, grad_v_self, grad_q_cross, grad_k_cross, grad_v_cross]
        )
        grad_out_all = jnp.stack([grad_o_self, grad_o_cross])
        grad_norm_all = jnp.stack([gain_g1, bias_g1, gain_g2, bias_g2, gain_g3, bias_g3])
        found = (grad_in_all, grad_out_all, grad_norm_all, grad_up, grad_down)
        return (jax.tree.map(jnp.add, totals, found), (block_out, tokens_grad))

    width = tokens.shape[1]
    count = tokens.shape[0] // SEQ
    items = (
        tokens.reshape(count, SEQ, width),
        memory.reshape(count, SEQ, width),
        cotangent.reshape(count, SEQ, width),
        lengths,
        breaks,
    )
    zeros_init = (
        jnp.zeros(in_rows.shape, jnp.float32),
        jnp.zeros(out_rows.shape, jnp.float32),
        jnp.zeros(norm_rows.shape, jnp.float32),
        jnp.zeros(up_rows.shape, jnp.float32),
        jnp.zeros(down_rows.shape, jnp.float32),
    )
    totals, (outs_all, grads_all) = lax.scan(protein_step, zeros_init, items)
    grad_in_all, grad_out_all, grad_norm_all, grad_up, grad_down = totals
    full_in, full_out, full_norm, full_up, full_down = lax.psum(
        (grad_in_all, grad_out_all, grad_norm_all, grad_up, grad_down), "dp"
    )
    owner = lax.axis_index("dp")
    own_rows = attn_in.shape[1]
    ffn_own = ffn_in.shape[0]
    shard_in = lax.dynamic_slice_in_dim(full_in, owner * own_rows, own_rows, 1)
    shard_out = lax.dynamic_slice_in_dim(full_out, owner * own_rows, own_rows, 1)
    shard_norm = lax.dynamic_slice_in_dim(full_norm, owner * norms.shape[1], norms.shape[1], 1)
    shard_up = lax.dynamic_slice_in_dim(full_up, owner * ffn_own, ffn_own, 0)
    shard_down = lax.dynamic_slice_in_dim(full_down, owner * ffn_own, ffn_own, 0)
    rate_scale = float(lax.axis_size("dp") * SEQ * count) ** (-0.5)
    in_g, in_m, in_w, in_a = update(
        attn_in, shard_in, attn_in_mom, attn_in_avg, BASE_RATES[0] * rate_scale
    )
    out_g, out_m, out_w, out_a = update(
        attn_out, shard_out, attn_out_mom, attn_out_avg, BASE_RATES[1] * rate_scale
    )
    up_g, up_m, up_w, up_a = update(
        ffn_in, shard_up, ffn_in_mom, ffn_in_avg, BASE_RATES[2] * rate_scale
    )
    down_g, down_m, down_w, down_a = update(
        ffn_out, shard_down, ffn_out_mom, ffn_out_avg, BASE_RATES[3] * rate_scale
    )
    norm_g, norm_m, norm_w, norm_a = update(
        norms, shard_norm, norms_mom, norms_avg, BASE_RATES[4] * rate_scale
    )
    return (
        outs_all.reshape(count * SEQ, width),
        grads_all.reshape(count * SEQ, width),
        in_g,
        in_m,
        in_w,
        in_a,
        out_g,
        out_m,
        out_w,
        out_a,
        up_g,
        up_m,
        up_w,
        up_a,
        down_g,
        down_m,
        down_w,
        down_a,
        norm_g,
        norm_m,
        norm_w,
        norm_a,
    )


def solution(mesh):
    return jax.shard_map(
        per_device,
        mesh=mesh,
        in_specs=(
            P("dp", None),
            P("dp", None),
            P("dp", None),
            P("dp"),
            P("dp"),
            P(None, "dp", "tensor"),
            P(None, "dp", "tensor"),
            P("dp", "tensor"),
            P("dp", "tensor"),
            P(None, "dp"),
            P(None, "dp", "tensor"),
            P(None, "dp", "tensor"),
            P("dp", "tensor"),
            P("dp", "tensor"),
            P(None, "dp"),
            P(None, "dp", "tensor"),
            P(None, "dp", "tensor"),
            P("dp", "tensor"),
            P("dp", "tensor"),
            P(None, "dp"),
        ),
        out_specs=(
            P("dp", None),
            P("dp", None),
            P(None, "dp", "tensor"),
            P(None, "dp", "tensor"),
            P(None, "dp", "tensor"),
            P(None, "dp", "tensor"),
            P(None, "dp", "tensor"),
            P(None, "dp", "tensor"),
            P(None, "dp", "tensor"),
            P(None, "dp", "tensor"),
            P("dp", "tensor"),
            P("dp", "tensor"),
            P("dp", "tensor"),
            P("dp", "tensor"),
            P("dp", "tensor"),
            P("dp", "tensor"),
            P("dp", "tensor"),
            P("dp", "tensor"),
            P(None, "dp"),
            P(None, "dp"),
            P(None, "dp"),
            P(None, "dp"),
        ),
        check_vma=False,
    )
```

profile of v0, /device:TPU:0, one launch (start us, length us, event | category | flops | bytes accessed | tf_op | source)
XLA Modules:
  0.0 873.6 jit_solution(5237097628865005914)
XLA Ops:
  8.9 27.8 %all-gather = bf16[8,64,6]{1,2,0:T(8,128)(2,1)S(1)} all-gather(bf16[1,64,6]{1,2,0:T(8,128)(2,1)S(1)} %convert_bitcast_fusion.1), channel_id=1, replica_groups=mesh['dp'=8,'tensor'=4] {'dp'}, dimensions={0}, use_global_device_ids=true | all-gather | bytes 6912 | tf_op jit(solution)/shard_map/all_gather | solution.py:138
  41.0 30.9 %all_gather.17 = bf16[2,512,128]{2,1,0:T(8,128)(2,1)S(1)} all-gather(bf16[2,64,128]{2,1,0:T(8,128)(2,1)S(1)} %convert_element_type.200), channel_id=1, replica_groups=mesh['dp'=8,'tensor'=4] {'dp'}, dimensions={1}, use_global_device_ids=true | all-gather | bytes 294912 | tf_op jit(solution)/shard_map/all_gather | solution.py:137
  71.8 33.4 %all_gather.19 = bf16[512,512]{1,0:T(8,128)(2,1)} all-gather(bf16[64,512]{1,0:T(8,128)(2,1)S(1)} %convert_element_type.202), channel_id=1, replica_groups=mesh['dp'=8,'tensor'=4] {'dp'}, dimensions={0}, use_global_device_ids=true | all-gather | bytes 589824 | tf_op jit(solution)/shard_map/all_gather | solution.py:142
  105.2 33.6 %all_gather.18 = bf16[512,512]{1,0:T(8,128)(2,1)} all-gather(bf16[64,512]{1,0:T(8,128)(2,1)S(1)} %convert_element_type.201), channel_id=1, replica_groups=mesh['dp'=8,'tensor'=4] {'dp'}, dimensions={0}, use_global_device_ids=true | all-gather | bytes 589824 | tf_op jit(solution)/shard_map/all_gather | solution.py:141
  138.7 33.6 %all_gather.16 = bf16[6,512,128]{2,1,0:T(8,128)(2,1)} all-gather(bf16[6,64,128]{2,1,0:T(8,128)(2,1)S(1)} %convert_element_type.199), channel_id=1, replica_groups=mesh['dp'=8,'tensor'=4] {'dp'}, dimensions={1}, use_global_device_ids=true | all-gather | bytes 884736 | tf_op jit(solution)/shard_map/all_gather | solution.py:136
  172.3 526.3 %while.23 = (s32[]{:T(128)}, f32[6,512,128]{2,1,0:T(8,128)}, f32[2,512,128]{2,1,0:T(8,128)}, f32[6,512]{1,0:T(8,128)}, f32[512,512]{1,0:T(8,128)}, /*index=5*/f3...) while((s32[]{:T(128)}, f32[6,512,128]{2,1,0:T(8,128)}, ...), condition=%wide.region_31.32_spmd.clone, body=%wide.region_0.31_spmd.clone.sunk | while | flops 3963490304 | bytes 262780928 | solution.py:243
  187.5 2.0 convolution_convert_fusion.30
  191.0 32.4 %all-reduce.13.cloned.1.call-done = f32[512,512]{1,0:T(8,128)} async-done(((f32[512,512]{1,0:T(8,128)}), f32[512,512]{1,0:T(8,128)}) %all-reduce.13.cloned.1.call-update) | async-done | bytes 1048592 | tf_op jit(solution)/shard_map/while/body/eval_jaxpr/psum | solution.py:148
  230.2 36.6 %all-reduce.15.cloned.1.call-done = f32[512,512]{1,0:T(8,128)} async-done(((f32[512,512]{1,0:T(8,128)}), f32[512,512]{1,0:T(8,128)}) %all-reduce.15.cloned.1.call-update) | async-done | bytes 1048592 | tf_op jit(solution)/shard_map/while/body/eval_jaxpr/psum | solution.py:148
  269.0 3.6 multiply_convert_fusion.6
  275.8 2.8 convolution_add_fusion.11
  281.9 30.5 %all-reduce.17.cloned.1.call-done = f32[512,512]{1,0:T(8,128)} async-done(((f32[512,512]{1,0:T(8,128)}), f32[512,512]{1,0:T(8,128)}) %all-reduce.17.cloned.1.call-update) | async-done | bytes 1048592 | tf_op jit(solution)/shard_map/while/body/eval_jaxpr/psum | solution.py:151
  312.4 2.5 multiply_reduce_fusion.19
  319.9 2.2 fusion.366
  322.2 2.4 fusion.373
  324.6 2.0 convolution_convert_fusion.35
  326.6 32.2 %all-reduce.19.cloned.1.call-done = f32[512,512]{1,0:T(8,128)} async-done(((f32[512,512]{1,0:T(8,128)}), f32[512,512]{1,0:T(8,128)}) %all-reduce.19.cloned.1.call-update) | async-done | bytes 1048592 | tf_op jit(solution)/shard_map/while/body/eval_jaxpr/psum | solution.py:151
  358.8 2.7 multiply_reduce_fusion.21
  372.2 2.2 convolution_add_fusion.9
  374.4 2.0 fusion.371
  378.3 2.1 fusion.374
  380.4 2.1 fusion.375
  382.7 3.0 select_add_fusion.4
  385.8 43.8 %all-reduce.21.cloned.1.call-done = (f32[512,512]{1,0:T(8,128)}, f32[512,512]{1,0:T(8,128)}) async-done(((f32[512,512]{1,0:T(8,128)}, f32[512,512]{1,0:T(8,128)}), (f32[512,512]{1,0:T(8,128)}, f32[512,512]{1,0:T(8,128)})) %all-reduce.21.cloned.1.call-update) | async-done | bytes 2097168 | tf_op jit(solution)/shard_map/while/body/eval_jaxpr/psum | solution.py:151
  429.6 2.1 fusion.378
  432.8 2.5 fusion.380
  450.5 2.0 convolution_convert_fusion.30
  453.9 32.9 %all-reduce.13.cloned.1.call-done = f32[512,512]{1,0:T(8,128)} async-done(((f32[512,512]{1,0:T(8,128)}), f32[512,512]{1,0:T(8,128)}) %all-reduce.13.cloned.1.call-update) | async-done | bytes 1048592 | tf_op jit(solution)/shard_map/while/body/eval_jaxpr/psum | solution.py:148
  493.6 36.6 %all-reduce.15.cloned.1.call-done = f32[512,512]{1,0:T(8,128)} async-done(((f32[512,512]{1,0:T(8,128)}), f32[512,512]{1,0:T(8,128)}) %all-reduce.15.cloned.1.call-update) | async-done | bytes 1048592 | tf_op jit(solution)/shard_map/while/body/eval_jaxpr/psum | solution.py:148
  532.3 3.6 multiply_convert_fusion.6
  539.2 3.2 convolution_add_fusion.11
  543.9 3.1 convolution_add_fusion.10
  546.9 28.8 %all-reduce.17.cloned.1.call-done = f32[512,512]{1,0:T(8,128)} async-done(((f32[512,512]{1,0:T(8,128)}), f32[512,512]{1,0:T(8,128)}) %all-reduce.17.cloned.1.call-update) | async-done | bytes 1048592 | tf_op jit(solution)/shard_map/while/body/eval_jaxpr/psum | solution.py:151
  575.7 2.5 multiply_reduce_fusion.19
  583.3 2.2 fusion.366
  585.6 2.4 fusion.373
  588.0 2.0 convolution_convert_fusion.35
  590.0 32.2 %all-reduce.19.cloned.1.call-done = f32[512,512]{1,0:T(8,128)} async-done(((f32[512,512]{1,0:T(8,128)}), f32[512,512]{1,0:T(8,128)}) %all-reduce.19.cloned.1.call-update) | async-done | bytes 1048592 | tf_op jit(solution)/shard_map/while/body/eval_jaxpr/psum | solution.py:151
  622.2 2.7 multiply_reduce_fusion.21
  635.5 2.2 convolution_add_fusion.9
  641.7 2.1 fusion.374
  643.8 2.1 fusion.375
  646.1 3.5 select_add_fusion.4
  649.6 43.3 %all-reduce.21.cloned.1.call-done = (f32[512,512]{1,0:T(8,128)}, f32[512,512]{1,0:T(8,128)}) async-done(((f32[512,512]{1,0:T(8,128)}, f32[512,512]{1,0:T(8,128)}), (f32[512,512]{1,0:T(8,128)}, f32[512,512]{1,0:T(8,128)})) %all-reduce.21.cloned.1.call-update) | async-done | bytes 2097168 | tf_op jit(solution)/shard_map/while/body/eval_jaxpr/psum | solution.py:151
  693.0 2.1 fusion.378
  696.1 2.5 fusion.380
  699.4 38.8 %psum.81 = f32[6,512]{1,0:T(8,128)S(1)} all-reduce(f32[6,512]{1,0:T(8,128)S(1)} %copy-done.60), channel_id=1, replica_groups=mesh['dp'=8,'tensor'=4] {'dp'}, use_global_device_ids=true, to_apply=%region_36.37 | all-reduce | flops 3072 | bytes 24576 | tf_op jit(solution)/shard_map/psum | solution.py:245
  738.9 121.8 %all-reduce.11.cloned.1.call-done = (f32[6,512,128]{2,1,0:T(8,128)}, f32[2,512,128]{2,1,0:T(8,128)}, f32[512,512]{1,0:T(8,128)}, f32[512,512]{1,0:T(8,128)}) async-done(((f32[6,512,128]{2,1,0:T(8,128)}, f32[2,512,128]{2,1,0:T(8,128)}, f32[512,512]{1,0:T(8,128)}, f32[512,512]{1,0:T(8,128)}), (f32[6,512,128]{2,1,0:T(8,128)}, f32[2,512,128]{2,1,0:T(8,128)}, f32[512,512]{1,0:T(8,128)}, ...) | async-done | bytes 4194320 | tf_op jit(solution)/shard_map/psum | solution.py:245
  (474 shorter events, 111.1 us)
Async XLA Ops:
  8.0 164.3 %copy-start.8 = (bf16[1024,512]{1,0:T(8,128)(2,1)S(1)}, bf16[1024,512]{1,0:T(8,128)(2,1)}, u32[]{:S(2)}) copy-start(bf16[1024,512]{1,0:T(8,128)(2,1)} %param.22) | copy-start | bytes 3145732
  172.3 51.0 %all-reduce.13.cloned.1.call-start = ((), (), s32[]{:S(2)}) async-start(), calls=%async_computation.1 | async-start | bytes 2097152 | tf_op jit(solution)/shard_map/while/body/eval_jaxpr/psum | solution.py:148
  172.8 12.0 %copy-start.46 = (f32[512]{0:T(512)}, f32[512]{0:T(512)S(1)}, u32[]{:S(2)}) copy-start(f32[512]{0:T(512)S(1)} %add_rsqrt_fusion.6) | copy-start | bytes 6148 | tf_op jit(solution)/shard_map/while
  174.4 10.4 %copy-start.48 = (f32[1,512]{1,0:T(1,128)}, f32[1,512]{1,0:T(1,128)S(1)}, u32[]{:S(2)}) copy-start(f32[1,512]{1,0:T(1,128)S(1)} %get-tuple-element.436) | copy-start | bytes 6148 | tf_op jit(solution)/shard_map/while
  174.4 50.7 %copy-start.50 = (f32[1,512]{1,0:T(1,128)}, f32[1,512]{1,0:T(1,128)S(1)}, u32[]{:S(2)}) copy-start(f32[1,512]{1,0:T(1,128)S(1)} %get-tuple-element.442) | copy-start | bytes 6148 | tf_op jit(solution)/shard_map/while
  176.0 9.1 %copy-start.20 = (bf16[512,128]{0,1:T(8,128)(2,1)}, bf16[512,128]{0,1:T(8,128)(2,1)S(1)}, u32[]{:S(2)}) copy-start(bf16[512,128]{0,1:T(8,128)(2,1)S(1)} %convolution_convert_fusion.26) | copy-start | bytes 393220 | tf_op jit(solution)/shard_map/while
  177.3 7.8 copy-start.42
  186.1 38.6 %copy-start.22 = (bf16[2,64,512]{2,1,0:T(8,128)(2,1)}, bf16[2,64,512]{2,1,0:T(8,128)(2,1)S(1)}, u32[]{:S(2)}) copy-start(bf16[2,64,512]{2,1,0:T(8,128)(2,1)S(1)} %convolution_convert_fusion.27) | copy-start | bytes 393220 | tf_op jit(solution)/shard_map/while
  187.5 79.3 %all-reduce.15.cloned.1.call-start = ((), (), s32[]{:S(2)}) async-start(), calls=%async_computation.2 | async-start | bytes 2097152 | tf_op jit(solution)/shard_map/while/body/eval_jaxpr/psum | solution.py:148
  230.2 82.2 %all-reduce.17.cloned.1.call-start = ((), (), s32[]{:S(2)}) async-start(), calls=%async_computation.3 | async-start | bytes 2097152 | tf_op jit(solution)/shard_map/while/body/eval_jaxpr/psum | solution.py:151
  275.7 83.1 %all-reduce.19.cloned.1.call-start = ((), (), s32[]{:S(2)}) async-start(), calls=%async_computation.4 | async-start | bytes 2097152 | tf_op jit(solution)/shard_map/while/body/eval_jaxpr/psum | solution.py:151
  322.2 107.4 %all-reduce.21.cloned.1.call-start = ((), (), s32[]{:S(2)}) async-start(), calls=%async_computation.5 | async-start | bytes 4194304 | tf_op jit(solution)/shard_map/while/body/eval_jaxpr/psum | solution.py:151
  326.6 34.9 %copy-start.3 = (f32[512,512]{1,0:T(8,128)S(1)}, f32[512,512]{1,0:T(8,128)}, u32[]{:S(2)}) copy-start(f32[512,512]{1,0:T(8,128)} %copy-done.2) | copy-start | bytes 3145732 | tf_op jit(solution)/shard_map/while
  326.6 34.9 %copy-start.51 = (f32[1,512]{1,0:T(1,128)S(1)}, f32[1,512]{1,0:T(1,128)}, u32[]{:S(2)}) copy-start(f32[1,512]{1,0:T(1,128)} %copy-done.50) | copy-start | bytes 6148 | tf_op jit(solution)/shard_map/while
  365.4 6.8 copy-start.18
  382.7 46.9 %copy-start.47 = (f32[512]{0:T(512)S(1)}, f32[512]{0:T(512)}, u32[]{:S(2)}) copy-start(f32[512]{0:T(512)} %copy-done.46) | copy-start | bytes 6148 | tf_op jit(solution)/shard_map/while
  382.7 46.9 %copy-start.49 = (f32[1,512]{1,0:T(1,128)S(1)}, f32[1,512]{1,0:T(1,128)}, u32[]{:S(2)}) copy-start(f32[1,512]{1,0:T(1,128)} %copy-done.48) | copy-start | bytes 6148 | tf_op jit(solution)/shard_map/while
  435.3 51.5 %all-reduce.13.cloned.1.call-start = ((), (), s32[]{:S(2)}) async-start(), calls=%async_computation.1 | async-start | bytes 2097152 | tf_op jit(solution)/shard_map/while/body/eval_jaxpr/psum | solution.py:148
  435.7 12.0 %copy-start.46 = (f32[512]{0:T(512)}, f32[512]{0:T(512)S(1)}, u32[]{:S(2)}) copy-start(f32[512]{0:T(512)S(1)} %add_rsqrt_fusion.6) | copy-start | bytes 6148 | tf_op jit(solution)/shard_map/while
  437.3 10.4 %copy-start.48 = (f32[1,512]{1,0:T(1,128)}, f32[1,512]{1,0:T(1,128)S(1)}, u32[]{:S(2)}) copy-start(f32[1,512]{1,0:T(1,128)S(1)} %get-tuple-element.436) | copy-start | bytes 6148 | tf_op jit(solution)/shard_map/while
  437.3 51.2 %copy-start.50 = (f32[1,512]{1,0:T(1,128)}, f32[1,512]{1,0:T(1,128)S(1)}, u32[]{:S(2)}) copy-start(f32[1,512]{1,0:T(1,128)S(1)} %get-tuple-element.442) | copy-start | bytes 6148 | tf_op jit(solution)/shard_map/while
  438.9 9.1 %copy-start.20 = (bf16[512,128]{0,1:T(8,128)(2,1)}, bf16[512,128]{0,1:T(8,128)(2,1)S(1)}, u32[]{:S(2)}) copy-start(bf16[512,128]{0,1:T(8,128)(2,1)S(1)} %convolution_convert_fusion.26) | copy-start | bytes 393220 | tf_op jit(solution)/shard_map/while
  440.2 7.8 copy-start.42
  449.1 39.1 %copy-start.22 = (bf16[2,64,512]{2,1,0:T(8,128)(2,1)}, bf16[2,64,512]{2,1,0:T(8,128)(2,1)S(1)}, u32[]{:S(2)}) copy-start(bf16[2,64,512]{2,1,0:T(8,128)(2,1)S(1)} %convolution_convert_fusion.27) | copy-start | bytes 393220 | tf_op jit(solution)/shard_map/while
  450.4 79.8 %all-reduce.15.cloned.1.call-start = ((), (), s32[]{:S(2)}) async-start(), calls=%async_computation.2 | async-start | bytes 2097152 | tf_op jit(solution)/shard_map/while/body/eval_jaxpr/psum | solution.py:148
  493.5 82.2 %all-reduce.17.cloned.1.call-start = ((), (), s32[]{:S(2)}) async-start(), calls=%async_computation.3 | async-start | bytes 2097152 | tf_op jit(solution)/shard_map/while/body/eval_jaxpr/psum | solution.py:151
  539.1 83.1 %all-reduce.19.cloned.1.call-start = ((), (), s32[]{:S(2)}) async-start(), calls=%async_computation.4 | async-start | bytes 2097152 | tf_op jit(solution)/shard_map/while/body/eval_jaxpr/psum | solution.py:151
  585.5 107.4 %all-reduce.21.cloned.1.call-start = ((), (), s32[]{:S(2)}) async-start(), calls=%async_computation.5 | async-start | bytes 4194304 | tf_op jit(solution)/shard_map/while/body/eval_jaxpr/psum | solution.py:151
  590.0 34.9 %copy-start.3 = (f32[512,512]{1,0:T(8,128)S(1)}, f32[512,512]{1,0:T(8,128)}, u32[]{:S(2)}) copy-start(f32[512,512]{1,0:T(8,128)} %copy-done.2) | copy-start | bytes 3145732 | tf_op jit(solution)/shard_map/while
  590.0 34.9 %copy-start.51 = (f32[1,512]{1,0:T(1,128)S(1)}, f32[1,512]{1,0:T(1,128)}, u32[]{:S(2)}) copy-start(f32[1,512]{1,0:T(1,128)} %copy-done.50) | copy-start | bytes 6148 | tf_op jit(solution)/shard_map/while
  646.1 46.9 %copy-start.47 = (f32[512]{0:T(512)S(1)}, f32[512]{0:T(512)}, u32[]{:S(2)}) copy-start(f32[512]{0:T(512)} %copy-done.46) | copy-start | bytes 6148 | tf_op jit(solution)/shard_map/while
  646.1 46.9 %copy-start.49 = (f32[1,512]{1,0:T(1,128)S(1)}, f32[1,512]{1,0:T(1,128)}, u32[]{:S(2)}) copy-start(f32[1,512]{1,0:T(1,128)} %copy-done.48) | copy-start | bytes 6148 | tf_op jit(solution)/shard_map/while
  698.6 162.1 %all-reduce.11.cloned.1.call-start = ((), (), s32[]{:S(2)}) async-start(), calls=%async_computation | async-start | bytes 8388608 | tf_op jit(solution)/shard_map/psum | solution.py:245
  698.7 39.6 %copy-start.81 = (f32[6,64]{1,0:T(8,128)S(1)}, f32[6,64]{1,0:T(8,128)}, u32[]{:S(2)}) copy-start(f32[6,64]{1,0:T(8,128)} %param.31) | copy-start | bytes 4612
  698.7 39.5 %copy-start.82 = (f32[6,64]{1,0:T(8,128)S(1)}, f32[6,64]{1,0:T(8,128)}, u32[]{:S(2)}) copy-start(f32[6,64]{1,0:T(8,128)} %param.41) | copy-start | bytes 4612
  698.7 39.5 %copy-start.83 = (f32[6,64]{1,0:T(8,128)S(1)}, f32[6,64]{1,0:T(8,128)}, u32[]{:S(2)}) copy-start(f32[6,64]{1,0:T(8,128)} %param.36) | copy-start | bytes 4612
  698.7 162.0 %copy-start.57 = (f32[6,64,128]{2,1,0:T(8,128)S(1)}, f32[6,64,128]{2,1,0:T(8,128)}, u32[]{:S(2)}) copy-start(f32[6,64,128]{2,1,0:T(8,128)} %param.27) | copy-start | bytes 589828
  698.7 162.0 %copy-start.71 = (f32[6,64,128]{2,1,0:T(8,128)S(1)}, f32[6,64,128]{2,1,0:T(8,128)}, u32[]{:S(2)}) copy-start(f32[6,64,128]{2,1,0:T(8,128)} %param.37) | copy-start | bytes 589828
  698.7 162.0 %copy-start.72 = (f32[6,64,128]{2,1,0:T(8,128)S(1)}, f32[6,64,128]{2,1,0:T(8,128)}, u32[]{:S(2)}) copy-start(f32[6,64,128]{2,1,0:T(8,128)} %param.32) | copy-start | bytes 589828
  698.7 163.8 %copy-start.64 = (f32[2,64,128]{2,1,0:T(8,128)S(1)}, f32[2,64,128]{2,1,0:T(8,128)}, u32[]{:S(2)}) copy-start(f32[2,64,128]{2,1,0:T(8,128)} %param.28) | copy-start | bytes 196612
  698.8 163.8 %copy-start.79 = (f32[2,64,128]{2,1,0:T(8,128)S(1)}, f32[2,64,128]{2,1,0:T(8,128)}, u32[]{:S(2)}) copy-start(f32[2,64,128]{2,1,0:T(8,128)} %param.38) | copy-start | bytes 196612
  698.8 163.8 %copy-start.80 = (f32[2,64,128]{2,1,0:T(8,128)S(1)}, f32[2,64,128]{2,1,0:T(8,128)}, u32[]{:S(2)}) copy-start(f32[2,64,128]{2,1,0:T(8,128)} %param.33) | copy-start | bytes 196612
  699.2 164.9 %copy-start.61 = (f32[64,512]{1,0:T(8,128)S(1)}, f32[64,512]{1,0:T(8,128)}, u32[]{:S(2)}) copy-start(f32[64,512]{1,0:T(8,128)} %param.29) | copy-start | bytes 393220
  699.2 164.9 %copy-start.62 = (f32[64,512]{1,0:T(8,128)S(1)}, f32[64,512]{1,0:T(8,128)}, u32[]{:S(2)}) copy-start(f32[64,512]{1,0:T(8,128)} %param.30) | copy-start | bytes 393220
  699.2 164.9 %copy-start.73 = (f32[64,512]{1,0:T(8,128)S(1)}, f32[64,512]{1,0:T(8,128)}, u32[]{:S(2)}) copy-start(f32[64,512]{1,0:T(8,128)} %param.40) | copy-start | bytes 393220
  699.2 164.9 %copy-start.74 = (f32[64,512]{1,0:T(8,128)S(1)}, f32[64,512]{1,0:T(8,128)}, u32[]{:S(2)}) copy-start(f32[64,512]{1,0:T(8,128)} %param.35) | copy-start | bytes 393220
  699.2 164.9 %copy-start.75 = (f32[64,512]{1,0:T(8,128)S(1)}, f32[64,512]{1,0:T(8,128)}, u32[]{:S(2)}) copy-start(f32[64,512]{1,0:T(8,128)} %param.34) | copy-start | bytes 393220
  699.3 164.9 %copy-start.76 = (f32[64,512]{1,0:T(8,128)S(1)}, f32[64,512]{1,0:T(8,128)}, u32[]{:S(2)}) copy-start(f32[64,512]{1,0:T(8,128)} %param.39) | copy-start | bytes 393220
  (114 other events, 308.3 us)
Sparse Core Ops, SparseCore 0:
  187.6 35.6 all-reduce.12
  230.3 36.4 all-reduce.14
  275.8 36.4 all-reduce.16
  322.3 36.4 all-reduce.18
  377.6 51.9 all-reduce.20
  450.5 36.1 all-reduce.12
  493.7 36.4 all-reduce.14
  539.2 36.4 all-reduce.16
  585.6 36.4 all-reduce.18
  640.9 51.9 all-reduce.20
Sparse Core Ops, SparseCore 1:
  703.1 157.6 all-reduce.10
where the time goes:
time: 875 us; the launch traced here: 874 us
  waiting for transfers between devices  471 us (54%)
  blocking collectives  198 us (23%)
  matrix products  104 us (12%)
  other arithmetic  61.3 us (7%)
  local copies, waits for them, and re-layouts  19.6 us (2%)
  between operations  15.7 us (2%)
    psum x6, waiting for transfers between devices, sum_grad(): return lax.psum(part_grad, 'tensor')  211 us
    psum x4, waiting for transfers between devices, add_branch(): return resid + lax.psum(part_out, 'tensor')  138 us
    psum x1, waiting for transfers between devices, per_device(): lax.psum((grad_in_all, grad_out_all, grad_norm_all, grad_up, grad_down),...  122 us
    psum x1, blocking collectives, per_device(): lax.psum((grad_in_all, grad_out_all, grad_norm_all, grad_up, grad_down),...  38.8 us
    dot_general x20, matrix products, weight_grad(): lax.dot_general(left_op, right_op, (((0,), (0,)), ((), ())), preferred_el...  33.7 us
    all_gather x1, blocking collectives, per_device(): lax.all_gather(attn_in.astype(low_type), 'dp', axis=1, tiled=True)  33.6 us
    all_gather x1, blocking collectives, per_device(): lax.all_gather(ffn_in.astype(low_type), 'dp', axis=0, tiled=True)  33.6 us
    all_gather x1, blocking collectives, per_device(): lax.all_gather(ffn_out.astype(low_type), 'dp', axis=0, tiled=True)  33.4 us
  transfers between devices with their start and end apart: 11, of which 11 were waited for; matrix products, arithmetic and copies ran while one was open for 5% of the time, Pallas kernels for 0%

commit v1 on v0

v1 whole, which is shorter than its diff:
```python
import functools

import jax
import jax.numpy as jnp
from jax import lax
from jax.experimental import pallas as pl
from jax.experimental.pallas import tpu as pltpu
from jax.sharding import PartitionSpec as P

HD = 64
SEQ = 512
WIDTH = 512
LINKER = 10
EPSILON = 1e-05
NEG_FILL = -1000000000.0
MOMENTUM = 0.9
AVG_DECAY = 0.6
BASE_RATES = (0.05, 1.0, 0.05, 0.05, 0.3)

BF = jnp.bfloat16
F32 = jnp.float32
MESH = pl.DeviceIdType.MESH
HEADS_HERE = 4
COLS = 256
BLOCKS = 16
GROUPS = 8
BLOCK_OF = (
    (0, 0), (0, 1), (0, 2), (1, 0),
    (0, 4), (0, 5), (0, 3), (1, 1),
    (2, 0), (3, 0), (2, 1), (3, 1),
    (2, 2), (3, 2), (2, 3), (3, 3),
)
WQ1, WK1, WV1, WO1, WK2, WV2, WQ2, WO2 = range(8)


def nn(left, right):
    return jnp.dot(left, right, preferred_element_type=F32)


def nt(left, right):
    return lax.dot_general(left, right, (((1,), (1,)), ((), ())), preferred_element_type=F32)


def layer_kernel(
    nz,
    tok_hbm, mem_hbm, cot_hbm, len_ref, brk_ref, ain, aout, fin, fout, norms,
    gsum, nsum, bout, tgrad,
    tok, mem, cot, W, G, R1A, R1B, R2, RZ, NB, NP, GAIN, NGR, NX, NY, NZB, NT,
    XS, XR, XF, XH, IV, OACC, DHA, H, HT, Q, K, V, KM, VM, PR, DS, A, DX, DQ, DK, DV,
    ACT, DU, DZ, DO, TR,
    lsem, ag_zs, ag_zr, ag_ms, ag_mr, nb_s, nb_r, xc_s, xc_r, rs_ms, rs_mr, rs_zs, rs_zr,
    ng_s, ng_r, out_s, out_r,
):
    dp, tensor = lax.axis_index("dp"), lax.axis_index("tensor")
    z, y, x, core = dp // 2, dp % 2, tensor // 2, tensor % 2
    rows_own = ain.shape[1]
    sibling = (dp, x * 2 + 1 - core)
    x_peer = (dp, (1 - x) * 2 + core)
    y_peer = (z * 2 + 1 - y, tensor)
    z_of = [None] + [lax.rem(z + step, nz) for step in range(1, nz)]
    z_peer = [None] + [(z_of[step] * 2 + y, tensor) for step in range(1, nz)]
    pending = []

    def send(src, dst, send_sem, recv_sem, peer):
        copy = pltpu.make_async_remote_copy(
            src, dst, send_sem, recv_sem, device_id=peer, device_id_type=MESH
        )
        copy.start()
        pending.append(copy)
        return copy

    barrier = pltpu.get_barrier_semaphore()
    peers = [sibling, x_peer, y_peer] + z_peer[1:]
    for peer in peers:
        pl.semaphore_signal(barrier, inc=1, device_id=peer, device_id_type=MESH)
    fetches = []
    for number, (src, dst) in enumerate(((tok_hbm, tok), (mem_hbm, mem), (cot_hbm, cot))):
        fetch = pltpu.make_async_copy(
            src.at[pl.ds(pl.multiple_of(x * SEQ, SEQ), SEQ)], dst, lsem.at[number]
        )
        fetch.start()
        fetches.append(fetch)

    NP[...] = jnp.zeros_like(NP)
    NP[0:6, 0:rows_own] = norms[...].astype(BF).astype(F32)
    lane_at = lax.rem(dp * rows_own, 128)
    NB[z, y] = pltpu.roll(NP[...], lane_at, 1)

    def own_block(arrays, block):
        array, index = BLOCK_OF[block]
        if array < 2:
            return arrays[array][index]
        return arrays[array][:, index * 128 : (index + 1) * 128]

    for block in range(BLOCKS):
        W[x, block, z, y] = own_block((ain, aout, fin, fout), block).astype(BF)
    pl.semaphore_wait(barrier, len(peers))

    ag_first, ag_second, ag_third, nb_first = {}, {}, {}, []

    def blocks_of(group):
        return pl.ds(2 * group, 2)

    def gather_start(group):
        part = W.at[x, blocks_of(group), z, y]
        ag_first[group] = [
            send(part, part, ag_zs.at[group, s - 1], ag_zr.at[group, s - 1], z_peer[s])
            for s in range(1, nz)
        ]

    def gather_mid(group):
        for copy in ag_first[group]:
            copy.wait_recv()
        part = W.at[x, blocks_of(group), :, y]
        peer = y_peer if group % 2 == 0 else x_peer
        ag_second[group] = send(part, part, ag_ms.at[0, group], ag_mr.at[0, group], peer)

    def gather_last(group):
        ag_second[group].wait_recv()
        if group % 2 == 0:
            part, peer = W.at[x, blocks_of(group)], x_peer
        else:
            part, peer = W.at[:, blocks_of(group), :, y], y_peer
        ag_third[group] = send(part, part, ag_ms.at[1, group], ag_mr.at[1, group], peer)

    def gather_done(group):
        ag_third[group].wait_recv()

    nb_first = [
        send(NB.at[z, y], NB.at[z, y], nb_s.at[s - 1], nb_r.at[s - 1], z_peer[s])
        for s in range(1, nz)
    ]
    for group in range(GROUPS):
        gather_start(group)

    def weight(block):
        return jnp.concatenate(
            [W[0, block].reshape(WIDTH, 128), W[1, block].reshape(WIDTH, 128)], axis=1
        )

    rs_first, rs_second, rs_third = {}, {}, {}

    def put_grad(block, value):
        low = value.astype(BF)
        G[0, block] = low[:, :128].reshape(G.shape[2:])
        G[1, block] = low[:, 128:].reshape(G.shape[2:])

    def sum_start(group):
        slot = pl.ds(2 * (group // 2), 2)
        if group % 2 == 0:
            src, dst, peer = G.at[1 - x, blocks_of(group)], R1A.at[slot], x_peer
        else:
            src, dst, peer = G.at[:, blocks_of(group), :, 1 - y], R1B.at[:, slot], y_peer
        rs_first[group] = send(src, dst, rs_ms.at[0, group], rs_mr.at[0, group], peer)

    def sum_mid(group):
        rs_first[group].wait_recv()
        for number in range(2):
            block, slot = 2 * group + number, 2 * (group // 2) + number
            if group % 2 == 0:
                G[x, block] = (G[x, block].astype(F32) + R1A[slot].astype(F32)).astype(BF)
            else:
                for side in range(2):
                    G[side, block, :, y] = (
                        G[side, block, :, y].astype(F32) + R1B[side, slot].astype(F32)
                    ).astype(BF)
        if group % 2 == 0:
            src, peer = G.at[x, blocks_of(group), :, 1 - y], y_peer
        else:
            src, peer = G.at[1 - x, blocks_of(group), :, y], x_peer
        rs_second[group] = send(
            src, R2.at[blocks_of(group)], rs_ms.at[1, group], rs_mr.at[1, group], peer
        )

    def sum_last(group):
        rs_second[group].wait_recv()
        for number in range(2):
            block = 2 * group + number
            G[x, block, :, y] = (
                G[x, block, :, y].astype(F32) + R2[block].astype(F32)
            ).astype(BF)
        rs_third[group] = [
            send(
                G.at[x, blocks_of(group), z_of[s], y],
                RZ.at[s - 1, blocks_of(group)],
                rs_zs.at[group, s - 1],
                rs_zr.at[group, s - 1],
                z_peer[s],
            )
            for s in range(1, nz)
        ]

    def sum_done(group):
        for copy in rs_third[group]:
            copy.wait_recv()
        for number in range(2):
            block = 2 * group + number
            total = G[x, block, z, y].astype(F32)
            for s in range(1, nz):
                total = total + RZ[s - 1, block].astype(F32)
            gsum[block] = total

    xc = {}

    def swap_start(number, half):
        rows = pl.ds(half * 256, 256)
        xc[number, half] = send(
            XS.at[number, rows],
            XR.at[number, rows],
            xc_s.at[number, half],
            xc_r.at[number, half],
            sibling,
        )

    def swap_sum(number, rows):
        return XS[number, rows].astype(F32) + XR[number, rows].astype(F32)

    def swap_rows(number, make):
        for half in range(2):
            rows = slice(half * 256, half * 256 + 256)
            XS[number, rows] = make(rows).astype(BF)
            swap_start(number, half)

    def each_rows(body, size=128, start=0, stop=SEQ):
        def one(step, carry):
            body(pl.ds(pl.multiple_of(start + step * size, size), size), start + step * size)
            return carry

        lax.fori_loop(0, (stop - start) // size, one, 0)

    def norm_rows(number, rows, values):
        center = values - jnp.mean(values, -1, keepdims=True)
        inv_std = lax.rsqrt(jnp.mean(center * center, -1, keepdims=True) + EPSILON)
        x_hat = center * inv_std
        XH[number, rows] = x_hat
        IV[number, rows] = inv_std
        gain, bias = GAIN[2 * number : 2 * number + 1], GAIN[2 * number + 1 : 2 * number + 2]
        H[number, rows] = (x_hat * gain + bias).astype(BF)

    def norm_back(number, rows, grad_h):
        x_hat, inv_std = XH[number, rows], IV[number, rows]
        NGR[2 * number] += jnp.sum((grad_h * x_hat).reshape(-1, 8, WIDTH), 0)
        NGR[2 * number + 1] += jnp.sum(grad_h.reshape(-1, 8, WIDTH), 0)
        grad_hat = grad_h * GAIN[2 * number : 2 * number + 1]
        return inv_std * (
            grad_hat
            - jnp.mean(grad_hat, -1, keepdims=True)
            - x_hat * jnp.mean(grad_hat * x_hat, -1, keepdims=True)
        )

    length_n, break_n = len_ref[x], brk_ref[x]

    def live_of(places):
        linker = (places >= break_n) & (places < break_n + LINKER)
        return (places < length_n) & jnp.logical_not(linker)

    def key_fill(count):
        places = lax.broadcasted_iota(jnp.int32, (1, count), 1)
        return jnp.where(live_of(places), 0.0, NEG_FILL)

    head_of = lax.broadcasted_iota(jnp.int32, (1, COLS), 1) // HD

    def split_heads(number):
        keys, values = K[number], V[number]
        for head in range(HEADS_HERE):
            KM[number, head] = jnp.where(head_of == head, keys, jnp.zeros_like(keys))
            VM[number, head] = jnp.where(head_of == head, values, jnp.zeros_like(values))

    def attend(number, half):
        count = 256 * (half + 1) if number == 0 else SEQ
        fill = key_fill(count)

        def body(rows, first):
            bias = fill
            if number == 0:
                row = first + lax.broadcasted_iota(jnp.int32, (128, count), 0)
                col = lax.broadcasted_iota(jnp.int32, (128, count), 1)
                bias = jnp.where(col <= row, fill, NEG_FILL)
            query = Q[number, rows]
            mixed = jnp.zeros((128, COLS), F32)
            for head in range(HEADS_HERE):
                scores = nt(query, KM[number, head, :count]) + bias
                expo = jnp.exp(scores - jnp.max(scores, -1, keepdims=True))
                prob = (expo * (1.0 / jnp.sum(expo, -1, keepdims=True))).astype(BF)
                PR[number, head, rows, :count] = prob
                mixed = mixed + nn(prob, VM[number, head, :count])
            A[number, rows] = mixed.astype(BF)

        each_rows(body, start=half * 256, stop=half * 256 + 256)

    def attend_back(number, half):
        count = 256 * (half + 1) if number == 0 else SEQ

        def body(rows, first):
            grad_o = DO[rows]
            grad_q = jnp.zeros((128, COLS), F32)
            for head in range(HEADS_HERE):
                grad_p = nt(grad_o, VM[number, head, :count])
                prob = PR[number, head, rows, :count].astype(F32)
                inner = jnp.sum(prob * grad_p, -1, keepdims=True)
                grad_s = (prob * (grad_p - inner)).astype(BF)
                DS[head, rows, :count] = grad_s
                grad_q = grad_q + nn(grad_s, KM[number, head, :count])
            DQ[rows] = (grad_q * HD**-0.5).astype(BF)

        each_rows(body, start=half * 256, stop=half * 256 + 256)

    def attend_keys(number):
        for table, source, target in ((PR.at[number], DO, DV), (DS, Q.at[number], DK)):
            source_t = source[...].T
            for head in range(HEADS_HERE):
                part = slice(head * HD, (head + 1) * HD)
                if number == 0:
                    TR[part, 0:256] = nn(source_t[part], table[head, :, 0:256]).astype(BF)
                    TR[part, 256:512] = nn(
                        source_t[part, 256:512], table[head, 256:512, 256:512]
                    ).astype(BF)
                else:
                    TR[part] = nn(source_t[part], table[head]).astype(BF)
            target[...] = TR[...].T

    for copy in nb_first:
        copy.wait_recv()
    nb_second = send(NB.at[:, y], NB.at[:, y], nb_s.at[nz - 1], nb_r.at[nz - 1], y_peer)
    gather_mid(0)
    gather_mid(1)
    nb_second.wait_recv()
    per_column = nz // 4
    for column in range(4):
        total = NB[column * per_column, 0] + NB[column * per_column, 1]
        for extra in range(1, per_column):
            total = total + NB[column * per_column + extra, 0] + NB[column * per_column + extra, 1]
        GAIN[:, column * 128 : (column + 1) * 128] = total
    NGR[...] = jnp.zeros_like(NGR)
    for fetch in fetches:
        fetch.wait()
    each_rows(lambda rows, first: norm_rows(0, rows, tok[rows].astype(F32)))
    HT[0] = H[0].T
    HT[1] = mem[...].T

    def dead_rows(rows, first):
        places = first + lax.broadcasted_iota(jnp.int32, (128, 1), 0)
        DZ[rows] = jnp.where(live_of(places), cot[rows].astype(F32), 0.0).astype(BF)

    each_rows(dead_rows)
    HT[4] = DZ[...].T
    gather_last(0)
    gather_last(1)
    gather_mid(2)
    gather_mid(3)
    gather_done(0)
    Q[0] = (nn(H[0], weight(WQ1)) * HD**-0.5).astype(BF)
    K[0] = nn(H[0], weight(WK1)).astype(BF)
    gather_done(1)
    V[0] = nn(H[0], weight(WV1)).astype(BF)
    gather_last(2)
    gather_last(3)
    split_heads(0)
    attend(0, 0)
    gather_mid(4)
    gather_mid(5)
    attend(0, 1)
    out_w = weight(WO1)
    swap_rows(0, lambda rows: nt(A[0, rows], out_w))
    gather_done(2)
    K[1] = nn(mem[...], weight(WK2)).astype(BF)
    V[1] = nn(mem[...], weight(WV2)).astype(BF)
    split_heads(1)
    gather_last(4)
    gather_last(5)

    def second_rows(rows, first):
        values = tok[rows].astype(F32) + swap_sum(0, rows)
        XF[rows] = values
        norm_rows(1, rows, values)

    xc[0, 0].wait_recv()
    xc[0, 1].wait_recv()
    each_rows(second_rows)
    gather_mid(6)
    gather_mid(7)
    gather_done(3)
    Q[1] = (nn(H[1], weight(WQ2)) * HD**-0.5).astype(BF)
    attend(1, 0)
    attend(1, 1)
    out_w = weight(WO2)
    swap_rows(1, lambda rows: nt(A[1, rows], out_w))
    gather_last(6)
    gather_last(7)
    HT[2] = H[1].T

    def third_rows(rows, first):
        values = XF[rows] + swap_sum(1, rows)
        XF[rows] = values
        norm_rows(2, rows, values)

    xc[1, 0].wait_recv()
    xc[1, 1].wait_recv()
    each_rows(third_rows)
    HT[3] = H[2].T

    for chunk in range(4):
        gather_done(4 + chunk)
        up, down = weight(8 + 2 * chunk), weight(9 + 2 * chunk)

        def hidden_rows(rows, first):
            hidden = nn(H[2, rows], up)
            grad_act = nn(DZ[rows], down)
            gate = 0.5 + 0.5 * lax.erf(hidden * 0.5**0.5)
            slope = gate + hidden * jnp.exp(-0.5 * hidden * hidden) * 0.3989422804014327
            act = (hidden * gate).astype(BF)
            grad_u = (grad_act * slope).astype(BF)
            ACT[rows] = act
            DU[rows] = grad_u
            if chunk == 0:
                OACC[rows] = nt(act, down)
                DHA[rows] = nt(grad_u, up)
            else:
                OACC[rows] += nt(act, down)
                DHA[rows] += nt(grad_u, up)

        each_rows(hidden_rows, size=256)
        put_grad(8 + 2 * chunk, nn(HT[3], DU[...]))
        put_grad(9 + 2 * chunk, nn(HT[4], ACT[...]))
        sum_start(4 + chunk)

    swap_rows(3, lambda rows: DHA[rows])
    swap_rows(2, lambda rows: OACC[rows])
    sum_mid(4)
    sum_mid(5)

    def back_third(rows, first):
        grad_out = DZ[rows].astype(F32)
        grad = grad_out + norm_back(2, rows, swap_sum(3, rows))
        DX[rows] = grad
        H[2, rows] = grad.astype(BF)

    xc[3, 0].wait_recv()
    xc[3, 1].wait_recv()
    each_rows(back_third)
    DO[...] = nn(H[2], weight(WO2)).astype(BF)
    put_grad(WO2, nn(H[2].T, A[1]))
    sum_mid(6)
    sum_mid(7)
    attend_back(1, 0)
    attend_back(1, 1)
    up = weight(WQ2)
    swap_rows(4, lambda rows: nt(DQ[rows], up))
    put_grad(WQ2, nn(HT[2], DQ[...]))
    sum_start(3)
    sum_last(4)
    sum_last(5)
    attend_keys(1)
    put_grad(WK2, nn(HT[1], DK[...]))
    put_grad(WV2, nn(HT[1], DV[...]))
    sum_start(2)

    def out_rows(rows, first):
        bout[x, rows] = (XF[rows] + swap_sum(2, rows)).astype(BF)

    half_own = pl.ds(pl.multiple_of(core * 256, 256), 256)

    def share_start(number, result):
        part = result.at[x, half_own]
        return send(part, part, out_s.at[number, 0], out_r.at[number, 0], x_peer)

    def share_pass(number, result):
        part = result.at[1 - x, half_own]
        return send(part, part, out_s.at[number, 1], out_r.at[number, 1], sibling)

    xc[2, 0].wait_recv()
    xc[2, 1].wait_recv()
    each_rows(out_rows)
    share_out = share_start(0, bout)

    def back_second(rows, first):
        grad = DX[rows] + norm_back(1, rows, swap_sum(4, rows))
        DX[rows] = grad
        H[2, rows] = grad.astype(BF)

    xc[4, 0].wait_recv()
    xc[4, 1].wait_recv()
    each_rows(back_second)
    DO[...] = nn(H[2], weight(WO1)).astype(BF)
    put_grad(WO1, nn(H[2].T, A[0]))
    sum_last(6)
    sum_last(7)
    attend_back(0, 0)
    sum_mid(3)
    attend_back(0, 1)
    sum_mid(2)
    attend_keys(0)
    put_grad(WV1, nn(HT[0], DV[...]))
    sum_start(1)
    put_grad(WQ1, nn(HT[0], DQ[...]))
    put_grad(WK1, nn(HT[0], DK[...]))
    sum_start(0)
    w_q, w_k, w_v = weight(WQ1), weight(WK1), weight(WV1)
    swap_rows(5, lambda rows: nt(DQ[rows], w_q) + nt(DK[rows], w_k) + nt(DV[rows], w_v))
    share_out.wait_recv()
    share_out2 = share_pass(0, bout)
    sum_last(3)
    sum_last(2)
    for group in (4, 5, 6, 7):
        sum_done(group)

    def back_first(rows, first):
        grad = DX[rows] + norm_back(0, rows, swap_sum(5, rows))
        tgrad[x, rows] = grad.astype(BF)

    xc[5, 0].wait_recv()
    xc[5, 1].wait_recv()
    each_rows(back_first)
    share_grad = share_start(1, tgrad)

    for row in range(6):
        NX[0, row : row + 1] = jnp.sum(NGR[row], 0, keepdims=True)
    NX[0, 6:8] = jnp.zeros((2, WIDTH), F32)
    norm_x = send(NX.at[0], NX.at[1], ng_s.at[0], ng_r.at[0], x_peer)
    sum_mid(1)
    norm_x.wait_recv()
    NY[0] = NX[0] + NX[1]
    norm_y = send(NY.at[0], NY.at[1], ng_s.at[1], ng_r.at[1], y_peer)
    sum_mid(0)
    sum_done(3)
    norm_y.wait_recv()
    NZB[nz - 1] = NY[0] + NY[1]
    norm_z = [
        send(NZB.at[nz - 1], NZB.at[s - 1], ng_s.at[1 + s], ng_r.at[1 + s], z_peer[s])
        for s in range(1, nz)
    ]
    sum_done(2)
    sum_last(1)
    sum_last(0)
    share_grad.wait_recv()
    share_grad2 = share_pass(1, tgrad)
    total = NZB[nz - 1]
    for s in range(1, nz):
        norm_z[s - 1].wait_recv()
        total = total + NZB[s - 1]
    NT[...] = total
    column = pl.ds(pl.multiple_of(dp * rows_own // 128 * 128, 128), 128)
    nsum[...] = pltpu.roll(NT[:, column], lax.rem(128 - lane_at, 128), 1)
    sum_done(1)
    sum_done(0)
    share_out2.wait_recv()
    share_grad2.wait_recv()
    for copy in pending:
        copy.wait_send()


def update(weight, grad, moment, average, rate):
    moment_new = MOMENTUM * moment + grad
    weight_new = weight - rate * (grad + MOMENTUM * moment_new)
    average_new = AVG_DECAY * average + (1.0 - AVG_DECAY) * weight_new
    return moment_new, weight_new, average_new


def update_kernel(rate_scale, gsum, nsum, tlow, *refs):
    weights, moments, averages, outs = refs[0:5], refs[5:10], refs[10:15], refs[15:]
    tgrad_out, results = outs[0], outs[1:]
    tgrad_out[...] = tlow[...].astype(F32)

    def one(which, at, grad):
        found = update(
            weights[which][at],
            grad,
            moments[which][at],
            averages[which][at],
            BASE_RATES[which] * rate_scale,
        )
        for number, value in enumerate((grad, *found)):
            results[4 * which + number][at] = value

    for block, (array, index) in enumerate(BLOCK_OF):
        at = (index,) if array < 2 else (slice(None), slice(index * 128, index * 128 + 128))
        one(array, at, gsum[block])
    wide = weights[4].shape[1]
    one(4, (slice(None), slice(None)), nsum[0:6, 0:wide])


def per_device(nz, *args):
    (tokens, memory, cotangent, lengths, breaks, attn_in, attn_out, ffn_in, ffn_out, norms) = args[:10]
    moments, averages = args[10:15], args[15:20]
    own = attn_in.shape[1]
    whole = (nz, 2, own, 128)
    vmem = pl.BlockSpec(memory_space=pltpu.VMEM)
    smem = pl.BlockSpec(memory_space=pltpu.SMEM)
    hbm = pl.BlockSpec(memory_space=pl.ANY)
    dma = pltpu.SemaphoreType.DMA

    def bf(*shape):
        return pltpu.VMEM(shape, BF)

    def f32(*shape):
        return pltpu.VMEM(shape, F32)

    scratch = [
        bf(SEQ, WIDTH), bf(SEQ, WIDTH), bf(SEQ, WIDTH),
        bf(2, BLOCKS, *whole), bf(2, BLOCKS, *whole),
        bf(8, *whole), bf(2, 8, nz, own, 128), bf(BLOCKS, nz, own, 128),
        bf(nz - 1, BLOCKS, own, 128),
        f32(nz, 2, 8, 128), f32(8, 128), f32(8, WIDTH),
        f32(6, 8, WIDTH), f32(2, 8, WIDTH), f32(2, 8, WIDTH), f32(nz, 8, WIDTH),
        f32(8, WIDTH),
        bf(6, SEQ, WIDTH), bf(6, SEQ, WIDTH),
        f32(SEQ, WIDTH), f32(3, SEQ, WIDTH), f32(3, SEQ, 1),
        f32(SEQ, WIDTH), f32(SEQ, WIDTH),
        bf(3, SEQ, WIDTH), bf(5, WIDTH, SEQ),
        bf(2, SEQ, COLS), bf(2, SEQ, COLS), bf(2, SEQ, COLS),
        bf(2, HEADS_HERE, SEQ, COLS), bf(2, HEADS_HERE, SEQ, COLS),
        bf(2, HEADS_HERE, SEQ, SEQ), bf(HEADS_HERE, SEQ, SEQ),
        bf(2, SEQ, COLS), f32(SEQ, WIDTH),
        bf(SEQ, COLS), bf(SEQ, COLS), bf(SEQ, COLS),
        bf(SEQ, COLS), bf(SEQ, COLS), bf(SEQ, WIDTH), bf(SEQ, COLS), bf(COLS, SEQ),
        dma((3,)), dma((GROUPS, nz - 1)), dma((GROUPS, nz - 1)),
        dma((2, GROUPS)), dma((2, GROUPS)), dma((nz,)), dma((nz,)),
        dma((6, 2)), dma((6, 2)),
        dma((2, GROUPS)), dma((2, GROUPS)), dma((GROUPS, nz - 1)), dma((GROUPS, nz - 1)),
        dma((nz + 1,)), dma((nz + 1,)), dma((2, 2)), dma((2, 2)),
    ]
    gsum, nsum, bout, tlow = pl.pallas_call(
        functools.partial(layer_kernel, nz),
        out_shape=(
            jax.ShapeDtypeStruct((BLOCKS, own, 128), F32),
            jax.ShapeDtypeStruct((8, 128), F32),
            jax.ShapeDtypeStruct((2, SEQ, WIDTH), BF),
            jax.ShapeDtypeStruct((2, SEQ, WIDTH), BF),
        ),
        in_specs=[hbm] * 3 + [smem] * 2 + [vmem] * 5,
        out_specs=(vmem,) * 4,
        scratch_shapes=scratch,
        compiler_params=pltpu.CompilerParams(
            collective_id=0, has_side_effects=True, vmem_limit_bytes=58 * 2**20
        ),
    )(tokens, memory, cotangent, lengths, breaks, attn_in, attn_out, ffn_in, ffn_out, norms)
    weights = (attn_in, attn_out, ffn_in, ffn_out, norms)
    rate_scale = float(lax.axis_size("dp") * tokens.shape[0]) ** -0.5
    results = pl.pallas_call(
        functools.partial(update_kernel, rate_scale),
        out_shape=(jax.ShapeDtypeStruct((2, SEQ, WIDTH), F32),)
        + tuple(jax.ShapeDtypeStruct(w.shape, F32) for w in weights for _ in range(4)),
        compiler_params=pltpu.CompilerParams(vmem_limit_bytes=32 * 2**20),
    )(gsum, nsum, tlow, *weights, *moments, *averages)
    return (bout.reshape(tokens.shape), results[0].reshape(tokens.shape), *results[1:])


def solution(mesh):
    rows, attn, ffn, norm = P("dp", None), P(None, "dp", "tensor"), P("dp", "tensor"), P(None, "dp")
    weights = (attn, attn, ffn, ffn, norm)
    return jax.shard_map(
        functools.partial(per_device, mesh.shape["dp"] // 2),
        mesh=mesh,
        in_specs=(rows, rows, rows, P("dp"), P("dp")) + weights * 3,
        out_specs=(rows, rows) + tuple(spec for spec in weights for _ in range(4)),
        check_vma=False,
    )
```

time: 875 us -> 121 us (0.14)
  waiting for transfers between devices: 471 us -> 0 us
  blocking collectives: 198 us -> 0 us
  Pallas kernels: 0 us -> 116 us
  matrix products: 104 us -> 0 us
  other arithmetic: 61.3 us -> 0 us
  local copies, waits for them, and re-layouts: 19.6 us -> 3.97 us
  between operations: 15.7 us -> 0.93 us
    psum x11 -> x0, waiting for transfers between devices: 471 us -> none  [the longest x6 211 us: sum_grad(): return lax.psum(part_grad, 'tensor')]
    all_gather x5 -> x0, blocking collectives: 159 us -> none  [the longest x1 33.6 us: per_device(): lax.all_gather(attn_in.astype(low_type), 'dp', axis=1, tiled=True)]
    pallas_call x0 -> x2, Pallas kernels: none -> 116 us  [the longest x1 114 us: per_device(): pl.pallas_call(functools.partial(layer_kernel, nz), out_shape=(jax.ShapeD...]
    dot_general x80 -> x0, matrix products: 104 us -> none  [the longest x20 33.7 us: weight_grad(): lax.dot_general(left_op, right_op, (((0,), (0,)), ((), ())), preferred_el...]
    psum x1 -> x0, blocking collectives: 38.8 us -> none  [per_device(): lax.psum((grad_in_all, grad_out_all, grad_norm_all, grad_up, grad_down),...]
    reduce_sum x22 -> x0, other arithmetic: 24 us -> none  [the longest x4 10.4 us: norm_back(): grad_gain = jnp.sum(grad_h * x_hat, 0)]
    add x18 -> x0, other arithmetic: 18.6 us -> none  [the longest x6 6.85 us: protein_step(): return (jax.tree.map(jnp.add, totals, found), (block_out, tokens_grad))]
    convert_element_type x15 -> x0, other arithmetic: 10.6 us -> none  [the longest x2 3.75 us: protein_step(): row_live = live.astype(jnp.float32)[:, None]]
  transfers between devices with their start and end apart: 11 -> 0, of which waited for: 11 -> 0; matrix products, arithmetic and copies ran while one was open for 5% -> 0% of each run, Pallas kernels for 0% -> 0%
where the time goes in v1:
time: 121 us
  Pallas kernels  116 us (96%)
  local copies, waits for them, and re-layouts  3.97 us (3%)
    pallas_call x1, Pallas kernels, per_device(): pl.pallas_call(functools.partial(layer_kernel, nz), out_shape=(jax.ShapeD...  114 us
    unnamed x39, local copies, waits for them, and re-layouts  3.97 us

profile of v1, /device:TPU:0, one launch (start us, length us, event | category | flops | bytes accessed | tf_op | source)
XLA Modules:
  0.0 120.7 jit_solution(10928578069217727279)
XLA Ops:
  0.7 0.0 copy-start.14
  0.7 0.0 copy-start.3
  0.7 0.0 copy-start.2
  0.7 0.0 copy-start.5
  0.7 0.0 copy-start.1
  0.7 0.0 copy-start.16
  0.7 0.0 copy-start.11
  0.7 0.0 copy-start.10
  0.7 0.0 copy-start.13
  0.8 0.0 copy-start.7
  0.8 0.0 copy-start.15
  0.8 0.0 copy-start.9
  0.8 0.0 copy-start.8
  0.8 0.0 copy-start.12
  0.8 0.0 copy-start.6
  0.8 113.6 %shard_map.363 = (f32[16,64,128]{2,1,0:T(8,128)}, f32[8,128]{1,0:T(8,128)}, bf16[2,512,512]{2,1,0:T(8,128)(2,1)}, bf16[2,512,512]{2,1,0:T(8,128)(2,1)}) custom-call(bf16[1024,512]{1,0:T(8,128)(2,1)} %tok_hbm.1, bf16[1024,512]{1,0:T(8,128)(2,1)} %mem_hbm.1, bf16[1024,512]{1,0:T(8,128)(2,1)} %cot_hbm.1, s32[2]{0:T(128)} %len_ref.1, s32[2]{0:T(128)} %brk_ref.1, ...), custom_call_target="tpu_custom_call" | custom-call | tf_op jit(solution)/shard_map/pallas_call | solution.py:622
  114.4 0.0 copy-done.14
  114.4 0.0 copy-done.3
  114.5 0.0 copy-done.2
  114.5 0.0 copy-done.5
  114.5 0.0 copy-done.1
  114.5 0.0 copy-done.16
  114.5 0.0 copy-done.11
  114.5 0.0 copy-done.10
  114.5 0.0 copy-done.13
  114.5 0.0 copy-done.7
  114.5 0.0 copy-done.15
  114.5 0.0 copy-done.9
  114.6 0.0 copy-done.8
  114.6 0.0 copy-done.12
  114.6 0.0 copy-done.6
  114.6 0.0 copy-start
  114.6 1.2 %copy-done = bf16[2,512,512]{2,1,0:T(8,128)(2,1)S(1)} copy-done((bf16[2,512,512]{2,1,0:T(8,128)(2,1)S(1)}, bf16[2,512,512]{2,1,0:T(8,128)(2,1)}, u32[]{:S(2)}) %copy-start) | copy-done | bytes 1048600
  115.8 0.0 copy-start.4
  115.8 1.0 copy-done.4
  116.9 0.0 copy-start.17
  116.9 0.7 copy-done.17
  117.5 0.0 copy-start.18
  117.5 2.2 %shard_map.364 = (f32[2,512,512]{2,1,0:T(8,128)}, f32[6,64,128]{2,1,0:T(8,128)}, f32[6,64,128]{2,1,0:T(8,128)}, f32[6,64,128]{2,1,0:T(8,128)}, f32[6,64,128]{2,1...) custom-call(f32[16,64,128]{2,1,0:T(8,128)S(1)} %copy-done.4, ...), custom_call_target="tpu_custom_call" | custom-call | tf_op jit(solution)/shard_map/pallas_call | solution.py:639
  119.8 0.0 copy-done.18
  119.8 1.0 copy.43
Async XLA Ops:
  0.7 113.8 %copy-start.14 = (f32[6,64]{1,0:T(8,128)S(1)}, f32[6,64]{1,0:T(8,128)}, u32[]{:S(2)}) copy-start(f32[6,64]{1,0:T(8,128)} %refs_4_.1) | copy-start | bytes 4612
  0.7 113.8 %copy-start.3 = (f32[64,512]{1,0:T(8,128)S(1)}, f32[64,512]{1,0:T(8,128)}, u32[]{:S(2)}) copy-start(f32[64,512]{1,0:T(8,128)} %refs_3_.1) | copy-start | bytes 393220
  0.7 113.8 %copy-start.2 = (f32[64,512]{1,0:T(8,128)S(1)}, f32[64,512]{1,0:T(8,128)}, u32[]{:S(2)}) copy-start(f32[64,512]{1,0:T(8,128)} %refs_2_.1) | copy-start | bytes 393220
  0.7 113.8 %copy-start.5 = (f32[2,64,128]{2,1,0:T(8,128)S(1)}, f32[2,64,128]{2,1,0:T(8,128)}, u32[]{:S(2)}) copy-start(f32[2,64,128]{2,1,0:T(8,128)} %refs_1_.1) | copy-start | bytes 196612
  0.7 113.8 %copy-start.1 = (f32[6,64,128]{2,1,0:T(8,128)S(1)}, f32[6,64,128]{2,1,0:T(8,128)}, u32[]{:S(2)}) copy-start(f32[6,64,128]{2,1,0:T(8,128)} %refs_0_.1) | copy-start | bytes 589828
  0.7 113.8 %copy-start.16 = (f32[6,64]{1,0:T(8,128)S(1)}, f32[6,64]{1,0:T(8,128)}, u32[]{:S(2)}) copy-start(f32[6,64]{1,0:T(8,128)} %refs_14_.1) | copy-start | bytes 4612
  0.7 113.8 %copy-start.11 = (f32[64,512]{1,0:T(8,128)S(1)}, f32[64,512]{1,0:T(8,128)}, u32[]{:S(2)}) copy-start(f32[64,512]{1,0:T(8,128)} %refs_13_.1) | copy-start | bytes 393220
  0.7 113.8 %copy-start.10 = (f32[64,512]{1,0:T(8,128)S(1)}, f32[64,512]{1,0:T(8,128)}, u32[]{:S(2)}) copy-start(f32[64,512]{1,0:T(8,128)} %refs_12_.1) | copy-start | bytes 393220
  0.7 113.8 %copy-start.13 = (f32[2,64,128]{2,1,0:T(8,128)S(1)}, f32[2,64,128]{2,1,0:T(8,128)}, u32[]{:S(2)}) copy-start(f32[2,64,128]{2,1,0:T(8,128)} %refs_11_.1) | copy-start | bytes 196612
  0.8 113.8 %copy-start.7 = (f32[6,64,128]{2,1,0:T(8,128)S(1)}, f32[6,64,128]{2,1,0:T(8,128)}, u32[]{:S(2)}) copy-start(f32[6,64,128]{2,1,0:T(8,128)} %refs_10_.1) | copy-start | bytes 589828
  0.8 113.8 %copy-start.15 = (f32[6,64]{1,0:T(8,128)S(1)}, f32[6,64]{1,0:T(8,128)}, u32[]{:S(2)}) copy-start(f32[6,64]{1,0:T(8,128)} %refs_9_.1) | copy-start | bytes 4612
  0.8 113.8 %copy-start.9 = (f32[64,512]{1,0:T(8,128)S(1)}, f32[64,512]{1,0:T(8,128)}, u32[]{:S(2)}) copy-start(f32[64,512]{1,0:T(8,128)} %refs_8_.1) | copy-start | bytes 393220
  0.8 113.8 %copy-start.8 = (f32[64,512]{1,0:T(8,128)S(1)}, f32[64,512]{1,0:T(8,128)}, u32[]{:S(2)}) copy-start(f32[64,512]{1,0:T(8,128)} %refs_7_.1) | copy-start | bytes 393220
  0.8 113.8 %copy-start.12 = (f32[2,64,128]{2,1,0:T(8,128)S(1)}, f32[2,64,128]{2,1,0:T(8,128)}, u32[]{:S(2)}) copy-start(f32[2,64,128]{2,1,0:T(8,128)} %refs_6_.1) | copy-start | bytes 196612
  0.8 113.8 %copy-start.6 = (f32[6,64,128]{2,1,0:T(8,128)S(1)}, f32[6,64,128]{2,1,0:T(8,128)}, u32[]{:S(2)}) copy-start(f32[6,64,128]{2,1,0:T(8,128)} %refs_5_.1) | copy-start | bytes 589828
  114.6 1.2 %copy-start = (bf16[2,512,512]{2,1,0:T(8,128)(2,1)S(1)}, bf16[2,512,512]{2,1,0:T(8,128)(2,1)}, u32[]{:S(2)}) copy-start(bf16[2,512,512]{2,1,0:T(8,128)(2,1)} %get-tuple-element.50.tlow) | copy-start | bytes 3145732
  115.8 1.0 copy-start.4
  116.9 0.7 copy-start.17
  117.5 2.2 %copy-start.18 = (bf16[2,512,512]{2,1,0:T(8,128)(2,1)S(1)}, bf16[2,512,512]{2,1,0:T(8,128)(2,1)}, u32[]{:S(2)}) copy-start(bf16[2,512,512]{2,1,0:T(8,128)(2,1)} %get-tuple-element.47) | copy-start | bytes 3145732

commit v2 on v1

v2 whole, which is shorter than its diff:
```python
import functools

import jax
import jax.numpy as jnp
from jax import lax
from jax.experimental import pallas as pl
from jax.experimental.pallas import tpu as pltpu
from jax.sharding import PartitionSpec as P

HD = 64
SEQ = 512
WIDTH = 512
LINKER = 10
EPSILON = 1e-05
NEG_FILL = -1000000000.0
MOMENTUM = 0.9
AVG_DECAY = 0.6
BASE_RATES = (0.05, 1.0, 0.05, 0.05, 0.3)

BF = jnp.bfloat16
F32 = jnp.float32
MESH = pl.DeviceIdType.MESH
HEADS_HERE = 4
COLS = 256
BLOCKS = 16
BLOCK_OF = (
    (0, 0), (0, 1), (0, 2), (1, 0),
    (0, 4), (0, 5), (0, 3), (1, 1),
    (2, 0), (3, 0), (2, 1), (3, 1),
    (2, 2), (3, 2), (2, 3), (3, 3),
)
WQ1, WK1, WV1, WO1, WK2, WV2, WQ2, WO2 = range(8)
GATHER = tuple((block, 1, ("zyx", "zxy")[block % 2]) for block in range(14)) + ((14, 1, "xyz"), (15, 1, "yxz"))
SUM = (
    (8, 1, "zyx"), (9, 1, "zxy"), (10, 1, "xyz"), (11, 1, "yxz"),
    (12, 1, "xyz"), (13, 1, "yxz"), (14, 1, "yzx"), (15, 1, "yxz"),
    (7, 1, "yzx"), (5, 1, "xyz"), (6, 1, "yxz"), (4, 1, "yxz"),
    (3, 1, "yzx"), (2, 1, "yxz"), (0, 1, "xyz"), (1, 1, "yxz"),
)


def nn(left, right):
    return jnp.dot(left, right, preferred_element_type=F32)


def nt(left, right):
    return lax.dot_general(left, right, (((1,), (1,)), ((), ())), preferred_element_type=F32)


def layer_kernel(
    nz,
    tok_hbm, mem_hbm, cot_hbm, len_ref, brk_ref, ain, aout, fin, fout, norms,
    gsum, nsum, bout, tgrad,
    tok, mem, cot, W, G, R, NB, NP, GAIN, NGR, NX, NY, NZB, NT,
    XS, XR, XF, XH, IV, OACC, DHA, H, HT, Q, K, V, KM, VM, PR, DS, A, DX, DQ, DK, DV,
    ACT, DU, DZ, DO, TR,
    lsem, ag_s, ag_r, rs_s, rs_r, nb_s, nb_r, xc_s, xc_r,
    ng_s, ng_r, out_s, out_r,
):
    dp, tensor = lax.axis_index("dp"), lax.axis_index("tensor")
    z, y, x, core = dp // 2, dp % 2, tensor // 2, tensor % 2
    rows_own = ain.shape[1]
    sibling = (dp, x * 2 + 1 - core)
    x_peer = (dp, (1 - x) * 2 + core)
    y_peer = (z * 2 + 1 - y, tensor)
    z_of = [None] + [lax.rem(z + step, nz) for step in range(1, nz)]
    z_peer = [None] + [(z_of[step] * 2 + y, tensor) for step in range(1, nz)]
    pending = []

    def send(src, dst, send_sem, recv_sem, peer, alone=True):
        copy = pltpu.make_async_remote_copy(
            src, dst, send_sem, recv_sem, device_id=peer, device_id_type=MESH
        )
        copy.start()
        if alone:
            pending.append(copy)
        return copy

    barrier = pltpu.get_barrier_semaphore()
    peers = [sibling, x_peer, y_peer] + z_peer[1:]
    for peer in peers:
        pl.semaphore_signal(barrier, inc=1, device_id=peer, device_id_type=MESH)
    fetches = []
    for number, (src, dst) in enumerate(((tok_hbm, tok), (mem_hbm, mem), (cot_hbm, cot))):
        fetch = pltpu.make_async_copy(
            src.at[pl.ds(pl.multiple_of(x * SEQ, SEQ), SEQ)], dst, lsem.at[number]
        )
        fetch.start()
        fetches.append(fetch)

    NP[...] = jnp.zeros_like(NP)
    NP[0:6, 0:rows_own] = norms[...].astype(BF).astype(F32)
    lane_at = lax.rem(dp * rows_own, 128)
    NB[z, y] = pltpu.roll(NP[...], lane_at, 1)

    def own_block(arrays, block):
        array, index = BLOCK_OF[block]
        if array < 2:
            return arrays[array][index]
        return arrays[array][:, index * 128 : (index + 1) * 128]

    for block in range(BLOCKS):
        W[x, block, z, y] = own_block((ain, aout, fin, fout), block).astype(BF)
    pl.semaphore_wait(barrier, len(peers))

    me_of = {"x": x, "y": y, "z": z}
    flights, nb_second = {}, []

    def send_all(key, axis, pieces, whole, sems):
        if axis == "z":
            copies = [(z_of[s], s - 1, z_peer[s]) for s in range(1, nz)]
        elif axis == "y":
            copies = [(1 - y, 0, y_peer)]
        else:
            copies = [(1 - x, 0, x_peer)]
        for place, slot, peer in copies:
            send(*pieces(place, slot), *sems, peer, False)
        flights[key] = pltpu.make_async_remote_copy(
            *whole, *sems, device_id=copies[0][2], device_id_type=MESH
        )
        pending.append(flights[key])

    def landed(key):
        flights[key].wait_recv()

    def place_of(done, blocks):
        at = {axis: slice(None) if axis in done else me_of[axis] for axis in "xyz"}
        return at, lambda: (at["x"], blocks, at["z"], at["y"])

    def gather(parcel, phase):
        if phase > 0:
            landed(("gather", parcel, phase - 1))
        if phase == 3:
            return
        first, count, route = GATHER[parcel]
        at, where = place_of(route[:phase], pl.ds(first, count))
        part = W.at[where()]
        sems = (ag_s.at[parcel, phase], ag_r.at[parcel, phase])
        if route[phase] == "z":
            at["z"] = pl.ds(0, nz - 1)
        much = W.at[where()]
        send_all(
            ("gather", parcel, phase), route[phase], lambda place, slot: (part, part), (much, much), sems
        )

    nb_first = [
        send(NB.at[z, y], NB.at[z, y], nb_s.at[s - 1], nb_r.at[s - 1], z_peer[s])
        for s in range(1, nz)
    ]

    def weight(block):
        return jnp.concatenate(
            [W[0, block].reshape(WIDTH, 128), W[1, block].reshape(WIDTH, 128)], axis=1
        )

    def put_grad(block, value):
        low = value.astype(BF)
        G[0, block] = low[:, :128].reshape(G.shape[2:])
        G[1, block] = low[:, 128:].reshape(G.shape[2:])

    def total(parcel, phase):
        first, count, route = SUM[parcel]
        if phase > 0:
            landed(("sum", parcel, phase - 1))
            into = R[parcel][phase - 1]
            left = [axis for axis in "xyz" if axis not in route[:phase]]
            at, _ = place_of([axis for axis in left], None)
            for number in range(count):
                for side in range(2) if "x" in left else (x,):
                    here = (side, first + number, at["z"], at["y"])
                    found = G[here].astype(F32)
                    for slot in range(nz - 1 if route[phase - 1] == "z" else 1):
                        landing = into[slot, side, number] if "x" in left else into[slot, number]
                        found = found + landing.astype(F32)
                    if phase == 3:
                        gsum[first + number] = found
                    else:
                        G[here] = found.astype(BF)
        if phase == 3:
            return
        axis, into = route[phase], R[parcel][phase]
        at, where = place_of([a for a in "xyz" if a not in route[:phase]], pl.ds(first, count))

        def pieces(place, slot):
            at[axis] = place
            return G.at[where()], into.at[slot]

        at[axis] = pl.ds(0, nz - 1) if axis == "z" else me_of[axis]
        much = G.at[where()]
        sems = (rs_s.at[parcel, phase], rs_r.at[parcel, phase])
        send_all(("sum", parcel, phase), axis, pieces, (much, into if axis == "z" else into.at[0]), sems)

    xc = {}

    def swap_start(number, half):
        rows = pl.ds(half * 256, 256)
        xc[number, half] = send(
            XS.at[number, rows],
            XR.at[number, rows],
            xc_s.at[number, half],
            xc_r.at[number, half],
            sibling,
        )

    def swap_sum(number, rows):
        return XS[number, rows].astype(F32) + XR[number, rows].astype(F32)

    def swap_rows(number, make):
        for half in range(2):
            rows = slice(half * 256, half * 256 + 256)
            XS[number, rows] = make(rows).astype(BF)
            swap_start(number, half)

    def each_rows(body, size=128, start=0, stop=SEQ):
        def one(step, carry):
            body(pl.ds(pl.multiple_of(start + step * size, size), size), start + step * size)
            return carry

        lax.fori_loop(0, (stop - start) // size, one, 0)

    def norm_rows(number, rows, values):
        center = values - jnp.mean(values, -1, keepdims=True)
        inv_std = lax.rsqrt(jnp.mean(center * center, -1, keepdims=True) + EPSILON)
        x_hat = center * inv_std
        XH[number, rows] = x_hat
        IV[number, rows] = inv_std
        gain, bias = GAIN[2 * number : 2 * number + 1], GAIN[2 * number + 1 : 2 * number + 2]
        H[number, rows] = (x_hat * gain + bias).astype(BF)

    def norm_back(number, rows, grad_h):
        x_hat, inv_std = XH[number, rows], IV[number, rows]
        NGR[2 * number] += jnp.sum((grad_h * x_hat).reshape(-1, 8, WIDTH), 0)
        NGR[2 * number + 1] += jnp.sum(grad_h.reshape(-1, 8, WIDTH), 0)
        grad_hat = grad_h * GAIN[2 * number : 2 * number + 1]
        return inv_std * (
            grad_hat
            - jnp.mean(grad_hat, -1, keepdims=True)
            - x_hat * jnp.mean(grad_hat * x_hat, -1, keepdims=True)
        )

    length_n, break_n = len_ref[x], brk_ref[x]

    def live_of(places):
        linker = (places >= break_n) & (places < break_n + LINKER)
        return (places < length_n) & jnp.logical_not(linker)

    def key_fill(count):
        places = lax.broadcasted_iota(jnp.int32, (1, count), 1)
        return jnp.where(live_of(places), 0.0, NEG_FILL)

    head_of = lax.broadcasted_iota(jnp.int32, (1, COLS), 1) // HD

    def split_heads(number):
        keys, values = K[number], V[number]
        for head in range(HEADS_HERE):
            KM[number, head] = jnp.where(head_of == head, keys, jnp.zeros_like(keys))
            VM[number, head] = jnp.where(head_of == head, values, jnp.zeros_like(values))

    def attend(number, half):
        count = 256 * (half + 1) if number == 0 else SEQ
        fill = key_fill(count)

        def body(rows, first):
            bias = fill
            if number == 0:
                row = first + lax.broadcasted_iota(jnp.int32, (128, count), 0)
                col = lax.broadcasted_iota(jnp.int32, (128, count), 1)
                bias = jnp.where(col <= row, fill, NEG_FILL)
            query = Q[number, rows]
            mixed = jnp.zeros((128, COLS), F32)
            for head in range(HEADS_HERE):
                scores = nt(query, KM[number, head, :count]) + bias
                expo = jnp.exp(scores - jnp.max(scores, -1, keepdims=True))
                prob = (expo * (1.0 / jnp.sum(expo, -1, keepdims=True))).astype(BF)
                PR[number, head, rows, :count] = prob
                mixed = mixed + nn(prob, VM[number, head, :count])
            A[number, rows] = mixed.astype(BF)

        each_rows(body, start=half * 256, stop=half * 256 + 256)

    def attend_back(number, half):
        count = 256 * (half + 1) if number == 0 else SEQ

        def body(rows, first):
            grad_o = DO[rows]
            grad_q = jnp.zeros((128, COLS), F32)
            for head in range(HEADS_HERE):
                grad_p = nt(grad_o, VM[number, head, :count])
                prob = PR[number, head, rows, :count].astype(F32)
                inner = jnp.sum(prob * grad_p, -1, keepdims=True)
                grad_s = (prob * (grad_p - inner)).astype(BF)
                DS[head, rows, :count] = grad_s
                grad_q = grad_q + nn(grad_s, KM[number, head, :count])
            DQ[rows] = (grad_q * HD**-0.5).astype(BF)

        each_rows(body, start=half * 256, stop=half * 256 + 256)

    def turned_product(number, table, source, target):
        source_t = source[...].T
        for head in range(HEADS_HERE):
            part = slice(head * HD, (head + 1) * HD)
            if number == 0:
                TR[part, 0:256] = nn(source_t[part], table[head, :, 0:256]).astype(BF)
                TR[part, 256:512] = nn(
                    source_t[part, 256:512], table[head, 256:512, 256:512]
                ).astype(BF)
            else:
                TR[part] = nn(source_t[part], table[head]).astype(BF)
        target[...] = TR[...].T

    def value_back(number):
        turned_product(number, PR.at[number], DO, DV)

    def key_back(number):
        turned_product(number, DS, Q.at[number], DK)

    def norms_pass():
        for copy in nb_first:
            copy.wait_recv()
        nb_second.append(send(NB.at[:, y], NB.at[:, y], nb_s.at[nz - 1], nb_r.at[nz - 1], y_peer))

    def gains():
        nb_second[0].wait_recv()
        per_column = nz // 4
        for column in range(4):
            first = column * per_column
            total = NB[first, 0] + NB[first, 1]
            for at in range(first + 1, first + per_column):
                total = total + NB[at, 0] + NB[at, 1]
            GAIN[:, column * 128 : (column + 1) * 128] = total
        NGR[...] = jnp.zeros_like(NGR)

    def fetched():
        for fetch in fetches:
            fetch.wait()

    def first_norm():
        each_rows(lambda rows, first: norm_rows(0, rows, tok[rows].astype(F32)))
        HT[0] = H[0].T

    def cotangent_rows():
        def dead_rows(rows, first):
            places = first + lax.broadcasted_iota(jnp.int32, (128, 1), 0)
            DZ[rows] = jnp.where(live_of(places), cot[rows].astype(F32), 0.0).astype(BF)

        each_rows(dead_rows)
        HT[4] = DZ[...].T

    def memory_turned():
        HT[1] = mem[...].T

    def self_queries():
        Q[0] = (nn(H[0], weight(WQ1)) * HD**-0.5).astype(BF)
        K[0] = nn(H[0], weight(WK1)).astype(BF)

    def self_values():
        V[0] = nn(H[0], weight(WV1)).astype(BF)
        split_heads(0)

    def project(number):
        out_w = weight(WO2 if number else WO1)
        swap_rows(number, lambda rows: nt(A[number, rows], out_w))

    def memory_keys():
        K[1] = nn(mem[...], weight(WK2)).astype(BF)
        V[1] = nn(mem[...], weight(WV2)).astype(BF)
        split_heads(1)

    def swapped(number):
        xc[number, 0].wait_recv()
        xc[number, 1].wait_recv()

    def second_norm():
        def second_rows(rows, first):
            values = tok[rows].astype(F32) + swap_sum(0, rows)
            XF[rows] = values
            norm_rows(1, rows, values)

        each_rows(second_rows)

    def cross_queries():
        Q[1] = (nn(H[1], weight(WQ2)) * HD**-0.5).astype(BF)

    def turn(number):
        HT[1 + number] = H[number].T

    def third_norm():
        def third_rows(rows, first):
            values = XF[rows] + swap_sum(1, rows)
            XF[rows] = values
            norm_rows(2, rows, values)

        each_rows(third_rows)

    def hidden_chunk(chunk):
        up, down = weight(8 + 2 * chunk), weight(9 + 2 * chunk)

        def hidden_rows(rows, first):
            hidden = nn(H[2, rows], up)
            grad_act = nn(DZ[rows], down)
            gate = 0.5 + 0.5 * lax.erf(hidden * 0.5**0.5)
            slope = gate + hidden * jnp.exp(-0.5 * hidden * hidden) * 0.3989422804014327
            act = (hidden * gate).astype(BF)
            grad_u = (grad_act * slope).astype(BF)
            ACT[rows] = act
            DU[rows] = grad_u
            if chunk == 0:
                OACC[rows] = nt(act, down)
                DHA[rows] = nt(grad_u, up)
            else:
                OACC[rows] += nt(act, down)
                DHA[rows] += nt(grad_u, up)

        each_rows(hidden_rows, size=256)

    def hidden_grads(chunk):
        put_grad(8 + 2 * chunk, nn(HT[3], DU[...]))
        put_grad(9 + 2 * chunk, nn(HT[4], ACT[...]))

    def hidden_swap():
        swap_rows(3, lambda rows: DHA[rows])

    def out_swap():
        swap_rows(2, lambda rows: OACC[rows])

    def back_third():
        def one(rows, first):
            grad = DZ[rows].astype(F32) + norm_back(2, rows, swap_sum(3, rows))
            DX[rows] = grad
            H[2, rows] = grad.astype(BF)

        each_rows(one)

    def back_second():
        def one(rows, first):
            grad = DX[rows] + norm_back(1, rows, swap_sum(4, rows))
            DX[rows] = grad
            H[2, rows] = grad.astype(BF)

        each_rows(one)

    def back_first():
        def one(rows, first):
            grad = DX[rows] + norm_back(0, rows, swap_sum(5, rows))
            tgrad[x, rows] = grad.astype(BF)

        each_rows(one)

    def project_back(number):
        block = WO2 if number else WO1
        DO[...] = nn(H[2], weight(block)).astype(BF)
        put_grad(block, nn(H[2].T, A[number]))

    def cross_query_back():
        up = weight(WQ2)
        swap_rows(4, lambda rows: nt(DQ[rows], up))

    def weight_grad(block, turned, grads):
        put_grad(block, nn(HT[turned], (DQ, DK, DV)[grads][...]))

    def self_back():
        w_q, w_k, w_v = weight(WQ1), weight(WK1), weight(WV1)
        swap_rows(5, lambda rows: nt(DQ[rows], w_q) + nt(DK[rows], w_k) + nt(DV[rows], w_v))

    half_own = pl.ds(pl.multiple_of(core * 256, 256), 256)
    shares = {}

    def share_start(number):
        part = (bout, tgrad)[number].at[x, half_own]
        shares[number, 0] = send(part, part, out_s.at[number, 0], out_r.at[number, 0], x_peer)

    def share_pass(number):
        shares[number, 0].wait_recv()
        part = (bout, tgrad)[number].at[1 - x, half_own]
        shares[number, 1] = send(part, part, out_s.at[number, 1], out_r.at[number, 1], sibling)

    def share_done(number):
        shares[number, 1].wait_recv()

    def out_rows():
        def one(rows, first):
            bout[x, rows] = (XF[rows] + swap_sum(2, rows)).astype(BF)

        each_rows(one)

    norm_sends = {}

    def norm_grads_start():
        for row in range(6):
            NX[0, row : row + 1] = jnp.sum(NGR[row], 0, keepdims=True)
        NX[0, 6:8] = jnp.zeros((2, WIDTH), F32)
        norm_sends["x"] = send(NX.at[0], NX.at[1], ng_s.at[0], ng_r.at[0], x_peer)

    def norm_grads_mid():
        norm_sends["x"].wait_recv()
        NY[0] = NX[0] + NX[1]
        norm_sends["y"] = send(NY.at[0], NY.at[1], ng_s.at[1], ng_r.at[1], y_peer)

    def norm_grads_last():
        norm_sends["y"].wait_recv()
        NZB[nz - 1] = NY[0] + NY[1]
        norm_sends["z"] = [
            send(NZB.at[nz - 1], NZB.at[s - 1], ng_s.at[1 + s], ng_r.at[1 + s], z_peer[s])
            for s in range(1, nz)
        ]

    def norm_grads_done():
        total = NZB[nz - 1]
        for s in range(1, nz):
            norm_sends["z"][s - 1].wait_recv()
            total = total + NZB[s - 1]
        NT[...] = total
        column = pl.ds(pl.multiple_of(dp * rows_own // 128 * 128, 128), 128)
        nsum[...] = pltpu.roll(NT[:, column], lax.rem(128 - lane_at, 128), 1)

    def finish():
        for copy in pending:
            copy.wait_send()

    plan = (
        (gather, 0, 0), (gather, 1, 0), (norms_pass,), (gather, 14, 0), (gather, 15, 0),
        (gather, 2, 0), (gather, 3, 0), (gather, 0, 1), (gather, 1, 1), (gather, 4, 0), (gather, 5, 0),
        (gains,), (fetched,), (first_norm,),
        (gather, 2, 1), (gather, 3, 1), (gather, 0, 2), (gather, 1, 2), (gather, 14, 1), (gather, 15, 1),
        (gather, 6, 0), (gather, 7, 0), (cotangent_rows,), (memory_turned,),
        (gather, 4, 1), (gather, 5, 1), (gather, 2, 2), (gather, 3, 2), (gather, 8, 0), (gather, 9, 0),
        (gather, 0, 3), (gather, 1, 3), (self_queries,),
        (gather, 6, 1), (gather, 7, 1), (gather, 4, 2), (gather, 5, 2), (gather, 10, 0), (gather, 11, 0),
        (gather, 2, 3), (self_values,), (attend, 0, 0),
        (gather, 8, 1), (gather, 9, 1), (gather, 6, 2), (gather, 7, 2), (gather, 12, 0), (gather, 13, 0),
        (attend, 0, 1), (gather, 3, 3), (project, 0),
        (gather, 10, 1), (gather, 11, 1), (gather, 8, 2), (gather, 9, 2),
        (gather, 4, 3), (gather, 5, 3), (memory_keys,), (gather, 14, 2), (gather, 15, 2),
        (swapped, 0), (second_norm,), (gather, 12, 1), (gather, 13, 1), (gather, 10, 2), (gather, 11, 2),
        (gather, 6, 3), (cross_queries,), (attend, 1, 0), (gather, 12, 2), (gather, 13, 2),
        (attend, 1, 1), (gather, 7, 3), (project, 1), (turn, 1), (swapped, 1), (third_norm,), (turn, 2),
        (gather, 8, 3), (gather, 9, 3), (hidden_chunk, 0), (hidden_grads, 0), (total, 0, 0), (total, 1, 0),
        (gather, 10, 3), (gather, 11, 3), (hidden_chunk, 1), (hidden_grads, 1), (total, 2, 0), (total, 3, 0),
        (gather, 12, 3), (gather, 13, 3), (hidden_chunk, 2), (hidden_grads, 2), (total, 4, 0), (total, 5, 0),
        (gather, 14, 3), (gather, 15, 3), (hidden_chunk, 3), (hidden_swap,),
        (hidden_grads, 3), (total, 6, 0), (total, 7, 0), (out_swap,),
        (total, 2, 1), (total, 3, 1),
        (swapped, 3), (back_third,), (project_back, 1), (total, 8, 0),
        (total, 4, 1), (total, 5, 1), (value_back, 1), (weight_grad, WV2, 1, 2), (total, 9, 0),
        (total, 0, 1), (total, 1, 1), (attend_back, 1, 0),
        (total, 6, 1), (total, 7, 1), (total, 2, 2), (total, 3, 2), (attend_back, 1, 1),
        (cross_query_back,), (weight_grad, WQ2, 2, 0), (total, 10, 0),
        (total, 4, 2), (total, 5, 2), (total, 8, 1), (total, 0, 2), (total, 1, 2),
        (key_back, 1), (weight_grad, WK2, 1, 1), (total, 11, 0), (total, 9, 1),
        (swapped, 2), (out_rows,), (share_start, 0),
        (swapped, 4), (back_second,), (project_back, 0), (total, 12, 0),
        (total, 6, 2), (total, 7, 2), (total, 10, 1), (value_back, 0), (weight_grad, WV1, 0, 2), (total, 13, 0),
        (total, 8, 2), (total, 9, 2), (attend_back, 0, 0), (total, 11, 1), (total, 10, 2),
        (total, 12, 1), (attend_back, 0, 1), (weight_grad, WQ1, 0, 0), (total, 14, 0),
        (total, 13, 1), (total, 11, 2),
        (key_back, 0), (weight_grad, WK1, 0, 1), (total, 15, 0), (self_back,),
        (total, 12, 2), (share_pass, 0), (total, 0, 3), (total, 1, 3), (total, 2, 3), (total, 3, 3),
        (swapped, 5), (back_first,), (share_start, 1), (norm_grads_start,), (total, 14, 1), (total, 13, 2),
        (total, 4, 3), (total, 5, 3), (total, 15, 1), (norm_grads_mid,),
        (total, 6, 3), (total, 7, 3), (total, 14, 2), (norm_grads_last,),
        (total, 8, 3), (total, 9, 3), (total, 15, 2), (share_pass, 1),
        (total, 10, 3), (total, 11, 3), (total, 12, 3), (norm_grads_done,),
        (total, 13, 3), (total, 14, 3), (total, 15, 3), (share_done, 0), (share_done, 1), (finish,),
    )
    for step, *of in plan:
        step(*of)


def update(weight, grad, moment, average, rate):
    moment_new = MOMENTUM * moment + grad
    weight_new = weight - rate * (grad + MOMENTUM * moment_new)
    average_new = AVG_DECAY * average + (1.0 - AVG_DECAY) * weight_new
    return moment_new, weight_new, average_new


def update_kernel(rate_scale, gsum, nsum, tlow, *refs):
    weights, moments, averages, outs = refs[0:5], refs[5:10], refs[10:15], refs[15:]
    tgrad_out, results = outs[0], outs[1:]
    tgrad_out[...] = tlow[...].astype(F32)

    def one(which, at, grad):
        found = update(
            weights[which][at],
            grad,
            moments[which][at],
            averages[which][at],
            BASE_RATES[which] * rate_scale,
        )
        for number, value in enumerate((grad, *found)):
            results[4 * which + number][at] = value

    for block, (array, index) in enumerate(BLOCK_OF):
        at = (index,) if array < 2 else (slice(None), slice(index * 128, index * 128 + 128))
        one(array, at, gsum[block])
    wide = weights[4].shape[1]
    one(4, (slice(None), slice(None)), nsum[0:6, 0:wide])


def per_device(nz, *args):
    (tokens, memory, cotangent, lengths, breaks, attn_in, attn_out, ffn_in, ffn_out, norms) = args[:10]
    moments, averages = args[10:15], args[15:20]
    own = attn_in.shape[1]
    whole = (nz, 2, own, 128)
    vmem = pl.BlockSpec(memory_space=pltpu.VMEM)
    smem = pl.BlockSpec(memory_space=pltpu.SMEM)
    hbm = pl.BlockSpec(memory_space=pl.ANY)
    dma = pltpu.SemaphoreType.DMA

    def bf(*shape):
        return pltpu.VMEM(shape, BF)

    def f32(*shape):
        return pltpu.VMEM(shape, F32)

    def landing(parcel, phase):
        _, count, route = parcel
        sizes = {"x": 2, "y": 2, "z": nz}
        left = [axis for axis in "xyz" if axis not in route[: phase + 1]]
        senders = nz - 1 if route[phase] == "z" else 1
        sides = [2] if "x" in left else []
        rest = [sizes[axis] for axis in "zy" if axis in left]
        return bf(senders, *sides, count, *rest, own, 128)

    landings = [[landing(parcel, phase) for phase in range(3)] for parcel in SUM]
    scratch = [
        bf(SEQ, WIDTH), bf(SEQ, WIDTH), bf(SEQ, WIDTH),
        bf(2, BLOCKS, *whole), bf(2, BLOCKS, *whole),
        landings,
        f32(nz, 2, 8, 128), f32(8, 128), f32(8, WIDTH),
        f32(6, 8, WIDTH), f32(2, 8, WIDTH), f32(2, 8, WIDTH), f32(nz, 8, WIDTH),
        f32(8, WIDTH),
        bf(6, SEQ, WIDTH), bf(6, SEQ, WIDTH),
        f32(SEQ, WIDTH), f32(3, SEQ, WIDTH), f32(3, SEQ, 1),
        f32(SEQ, WIDTH), f32(SEQ, WIDTH),
        bf(3, SEQ, WIDTH), bf(5, WIDTH, SEQ),
        bf(2, SEQ, COLS), bf(2, SEQ, COLS), bf(2, SEQ, COLS),
        bf(2, HEADS_HERE, SEQ, COLS), bf(2, HEADS_HERE, SEQ, COLS),
        bf(2, HEADS_HERE, SEQ, SEQ), bf(HEADS_HERE, SEQ, SEQ),
        bf(2, SEQ, COLS), f32(SEQ, WIDTH),
        bf(SEQ, COLS), bf(SEQ, COLS), bf(SEQ, COLS),
        bf(SEQ, COLS), bf(SEQ, COLS), bf(SEQ, WIDTH), bf(SEQ, COLS), bf(COLS, SEQ),
        dma((3,)), *[dma((len(GATHER), 3))] * 2, *[dma((len(SUM), 3))] * 2,
        dma((nz,)), dma((nz,)),
        dma((6, 2)), dma((6, 2)),
        dma((nz + 1,)), dma((nz + 1,)), dma((2, 2)), dma((2, 2)),
    ]
    gsum, nsum, bout, tlow = pl.pallas_call(
        functools.partial(layer_kernel, nz),
        out_shape=(
            jax.ShapeDtypeStruct((BLOCKS, own, 128), F32),
            jax.ShapeDtypeStruct((8, 128), F32),
            jax.ShapeDtypeStruct((2, SEQ, WIDTH), BF),
            jax.ShapeDtypeStruct((2, SEQ, WIDTH), BF),
        ),
        in_specs=[hbm] * 3 + [smem] * 2 + [vmem] * 5,
        out_specs=(vmem,) * 4,
        scratch_shapes=scratch,
        compiler_params=pltpu.CompilerParams(
            collective_id=0, has_side_effects=True, vmem_limit_bytes=58 * 2**20
        ),
    )(tokens, memory, cotangent, lengths, breaks, attn_in, attn_out, ffn_in, ffn_out, norms)
    weights = (attn_in, attn_out, ffn_in, ffn_out, norms)
    rate_scale = float(lax.axis_size("dp") * tokens.shape[0]) ** -0.5
    results = pl.pallas_call(
        functools.partial(update_kernel, rate_scale),
        out_shape=(jax.ShapeDtypeStruct((2, SEQ, WIDTH), F32),)
        + tuple(jax.ShapeDtypeStruct(w.shape, F32) for w in weights for _ in range(4)),
        compiler_params=pltpu.CompilerParams(vmem_limit_bytes=32 * 2**20),
    )(gsum, nsum, tlow, *weights, *moments, *averages)
    return (bout.reshape(tokens.shape), results[0].reshape(tokens.shape), *results[1:])


def solution(mesh):
    rows, attn, ffn, norm = P("dp", None), P(None, "dp", "tensor"), P("dp", "tensor"), P(None, "dp")
    weights = (attn, attn, ffn, ffn, norm)
    return jax.shard_map(
        functools.partial(per_device, mesh.shape["dp"] // 2),
        mesh=mesh,
        in_specs=(rows, rows, rows, P("dp"), P("dp")) + weights * 3,
        out_specs=(rows, rows) + tuple(spec for spec in weights for _ in range(4)),
        check_vma=False,
    )
```

time: 121 us -> 113 us (0.934)
  Pallas kernels: 116 us -> 108 us
    pallas_call x1, Pallas kernels: 114 us -> 106 us  [per_device(): pl.pallas_call(functools.partial(layer_kernel, nz), out_shape=(jax.ShapeD...]
where the time goes in v2:
time: 113 us
  Pallas kernels  108 us (96%)
  local copies, waits for them, and re-layouts  3.97 us (4%)
    pallas_call x1, Pallas kernels, per_device(): pl.pallas_call(functools.partial(layer_kernel, nz), out_shape=(jax.ShapeD...  106 us
    unnamed x39, local copies, waits for them, and re-layouts  3.97 us

profile of v2, /device:TPU:0, one launch (start us, length us, event | category | flops | bytes accessed | tf_op | source)
XLA Modules:
  0.0 113.0 jit_solution(17774911075111420620)
XLA Ops:
  0.7 0.0 copy-start.14
  0.7 0.0 copy-start.3
  0.7 0.0 copy-start.2
  0.7 0.0 copy-start.5
  0.7 0.0 copy-start.1
  0.7 0.0 copy-start.16
  0.7 0.0 copy-start.11
  0.7 0.0 copy-start.10
  0.7 0.0 copy-start.13
  0.8 0.0 copy-start.7
  0.8 0.0 copy-start.15
  0.8 0.0 copy-start.9
  0.8 0.0 copy-start.8
  0.8 0.0 copy-start.12
  0.8 0.0 copy-start.6
  0.8 105.9 %shard_map.363 = (f32[16,64,128]{2,1,0:T(8,128)}, f32[8,128]{1,0:T(8,128)}, bf16[2,512,512]{2,1,0:T(8,128)(2,1)}, bf16[2,512,512]{2,1,0:T(8,128)(2,1)}) custom-call(bf16[1024,512]{1,0:T(8,128)(2,1)} %tok_hbm.1, bf16[1024,512]{1,0:T(8,128)(2,1)} %mem_hbm.1, bf16[1024,512]{1,0:T(8,128)(2,1)} %cot_hbm.1, s32[2]{0:T(128)} %len_ref.1, s32[2]{0:T(128)} %brk_ref.1, ...), custom_call_target="tpu_custom_call" | custom-call | tf_op jit(solution)/shard_map/pallas_call | solution.py:647
  106.7 0.0 copy-done.14
  106.7 0.0 copy-done.3
  106.7 0.0 copy-done.2
  106.7 0.0 copy-done.5
  106.7 0.0 copy-done.1
  106.7 0.0 copy-done.16
  106.7 0.0 copy-done.11
  106.8 0.0 copy-done.10
  106.8 0.0 copy-done.13
  106.8 0.0 copy-done.7
  106.8 0.0 copy-done.15
  106.8 0.0 copy-done.9
  106.8 0.0 copy-done.8
  106.8 0.0 copy-done.12
  106.8 0.0 copy-done.6
  106.8 0.0 copy-start
  106.8 1.2 %copy-done = bf16[2,512,512]{2,1,0:T(8,128)(2,1)S(1)} copy-done((bf16[2,512,512]{2,1,0:T(8,128)(2,1)S(1)}, bf16[2,512,512]{2,1,0:T(8,128)(2,1)}, u32[]{:S(2)}) %copy-start) | copy-done | bytes 1048600
  108.1 0.0 copy-start.4
  108.1 1.0 copy-done.4
  109.1 0.0 copy-start.17
  109.1 0.7 copy-done.17
  109.8 0.0 copy-start.18
  109.8 2.2 %shard_map.364 = (f32[2,512,512]{2,1,0:T(8,128)}, f32[6,64,128]{2,1,0:T(8,128)}, f32[6,64,128]{2,1,0:T(8,128)}, f32[6,64,128]{2,1,0:T(8,128)}, f32[6,64,128]{2,1...) custom-call(f32[16,64,128]{2,1,0:T(8,128)S(1)} %copy-done.4, ...), custom_call_target="tpu_custom_call" | custom-call | tf_op jit(solution)/shard_map/pallas_call | solution.py:664
  112.0 0.0 copy-done.18
  112.0 1.0 copy.43
Async XLA Ops:
  0.7 106.0 %copy-start.14 = (f32[6,64]{1,0:T(8,128)S(1)}, f32[6,64]{1,0:T(8,128)}, u32[]{:S(2)}) copy-start(f32[6,64]{1,0:T(8,128)} %refs_4_.1) | copy-start | bytes 4612
  0.7 106.0 %copy-start.3 = (f32[64,512]{1,0:T(8,128)S(1)}, f32[64,512]{1,0:T(8,128)}, u32[]{:S(2)}) copy-start(f32[64,512]{1,0:T(8,128)} %refs_3_.1) | copy-start | bytes 393220
  0.7 106.0 %copy-start.2 = (f32[64,512]{1,0:T(8,128)S(1)}, f32[64,512]{1,0:T(8,128)}, u32[]{:S(2)}) copy-start(f32[64,512]{1,0:T(8,128)} %refs_2_.1) | copy-start | bytes 393220
  0.7 106.0 %copy-start.5 = (f32[2,64,128]{2,1,0:T(8,128)S(1)}, f32[2,64,128]{2,1,0:T(8,128)}, u32[]{:S(2)}) copy-start(f32[2,64,128]{2,1,0:T(8,128)} %refs_1_.1) | copy-start | bytes 196612
  0.7 106.0 %copy-start.1 = (f32[6,64,128]{2,1,0:T(8,128)S(1)}, f32[6,64,128]{2,1,0:T(8,128)}, u32[]{:S(2)}) copy-start(f32[6,64,128]{2,1,0:T(8,128)} %refs_0_.1) | copy-start | bytes 589828
  0.7 106.0 %copy-start.16 = (f32[6,64]{1,0:T(8,128)S(1)}, f32[6,64]{1,0:T(8,128)}, u32[]{:S(2)}) copy-start(f32[6,64]{1,0:T(8,128)} %refs_14_.1) | copy-start | bytes 4612
  0.7 106.0 %copy-start.11 = (f32[64,512]{1,0:T(8,128)S(1)}, f32[64,512]{1,0:T(8,128)}, u32[]{:S(2)}) copy-start(f32[64,512]{1,0:T(8,128)} %refs_13_.1) | copy-start | bytes 393220
  0.7 106.0 %copy-start.10 = (f32[64,512]{1,0:T(8,128)S(1)}, f32[64,512]{1,0:T(8,128)}, u32[]{:S(2)}) copy-start(f32[64,512]{1,0:T(8,128)} %refs_12_.1) | copy-start | bytes 393220
  0.7 106.0 %copy-start.13 = (f32[2,64,128]{2,1,0:T(8,128)S(1)}, f32[2,64,128]{2,1,0:T(8,128)}, u32[]{:S(2)}) copy-start(f32[2,64,128]{2,1,0:T(8,128)} %refs_11_.1) | copy-start | bytes 196612
  0.8 106.0 %copy-start.7 = (f32[6,64,128]{2,1,0:T(8,128)S(1)}, f32[6,64,128]{2,1,0:T(8,128)}, u32[]{:S(2)}) copy-start(f32[6,64,128]{2,1,0:T(8,128)} %refs_10_.1) | copy-start | bytes 589828
  0.8 106.0 %copy-start.15 = (f32[6,64]{1,0:T(8,128)S(1)}, f32[6,64]{1,0:T(8,128)}, u32[]{:S(2)}) copy-start(f32[6,64]{1,0:T(8,128)} %refs_9_.1) | copy-start | bytes 4612
  0.8 106.0 %copy-start.9 = (f32[64,512]{1,0:T(8,128)S(1)}, f32[64,512]{1,0:T(8,128)}, u32[]{:S(2)}) copy-start(f32[64,512]{1,0:T(8,128)} %refs_8_.1) | copy-start | bytes 393220
  0.8 106.0 %copy-start.8 = (f32[64,512]{1,0:T(8,128)S(1)}, f32[64,512]{1,0:T(8,128)}, u32[]{:S(2)}) copy-start(f32[64,512]{1,0:T(8,128)} %refs_7_.1) | copy-start | bytes 393220
  0.8 106.0 %copy-start.12 = (f32[2,64,128]{2,1,0:T(8,128)S(1)}, f32[2,64,128]{2,1,0:T(8,128)}, u32[]{:S(2)}) copy-start(f32[2,64,128]{2,1,0:T(8,128)} %refs_6_.1) | copy-start | bytes 196612
  0.8 106.0 %copy-start.6 = (f32[6,64,128]{2,1,0:T(8,128)S(1)}, f32[6,64,128]{2,1,0:T(8,128)}, u32[]{:S(2)}) copy-start(f32[6,64,128]{2,1,0:T(8,128)} %refs_5_.1) | copy-start | bytes 589828
  106.8 1.2 %copy-start = (bf16[2,512,512]{2,1,0:T(8,128)(2,1)S(1)}, bf16[2,512,512]{2,1,0:T(8,128)(2,1)}, u32[]{:S(2)}) copy-start(bf16[2,512,512]{2,1,0:T(8,128)(2,1)} %get-tuple-element.50.tlow) | copy-start | bytes 3145732
  108.1 1.0 copy-start.4
  109.1 0.7 copy-start.17
  109.8 2.2 %copy-start.18 = (bf16[2,512,512]{2,1,0:T(8,128)(2,1)S(1)}, bf16[2,512,512]{2,1,0:T(8,128)(2,1)}, u32[]{:S(2)}) copy-start(bf16[2,512,512]{2,1,0:T(8,128)(2,1)} %get-tuple-element.47) | copy-start | bytes 3145732

commit v3 on v2

--- a/solution.py
+++ b/solution.py
@@ -32,10 +32,10 @@
 WQ1, WK1, WV1, WO1, WK2, WV2, WQ2, WO2 = range(8)
 GATHER = tuple((block, 1, ("zyx", "zxy")[block % 2]) for block in range(14)) + ((14, 1, "xyz"), (15, 1, "yxz"))
 SUM = (
-    (8, 1, "zyx"), (9, 1, "zxy"), (10, 1, "xyz"), (11, 1, "yxz"),
-    (12, 1, "xyz"), (13, 1, "yxz"), (14, 1, "yzx"), (15, 1, "yxz"),
-    (7, 1, "yzx"), (5, 1, "xyz"), (6, 1, "yxz"), (4, 1, "yxz"),
-    (3, 1, "yzx"), (2, 1, "yxz"), (0, 1, "xyz"), (1, 1, "yxz"),
+    (8, 1, "zxy"), (9, 1, "zxy"), (10, 1, "yzx"), (11, 1, "xyz"),
+    (12, 1, "yxz"), (13, 1, "yxz"), (14, 1, "xzy"), (15, 1, "yxz"),
+    (7, 1, "yzx"), (5, 1, "yxz"), (6, 1, "xyz"), (4, 1, "xyz"),
+    (3, 1, "xzy"), (2, 1, "yzx"), (0, 1, "yzx"), (1, 1, "yxz"),
 )
 
 
@@ -49,9 +49,9 @@
 
 def layer_kernel(
     nz,
-    tok_hbm, mem_hbm, cot_hbm, len_ref, brk_ref, ain, aout, fin, fout, norms,
-    gsum, nsum, bout, tgrad,
-    tok, mem, cot, W, G, R, NB, NP, GAIN, NGR, NX, NY, NZB, NT,
+    tok_hbm, mem_hbm, cot_hbm, len_ref, brk_ref, ain_hbm, aout_hbm, fin_hbm, fout_hbm, norms_hbm,
+    gsum_hbm, nsum_hbm, bout_hbm, tgrad_hbm,
+    gsum, nsum, bout, tgrad, ain, aout, fin, fout, norms, tok, mem, cot, W, G, R, NB, NP, GAIN, NGR, NX, NY, NZB, NT,
     XS, XR, XF, XH, IV, OACC, DHA, H, HT, Q, K, V, KM, VM, PR, DS, A, DX, DQ, DK, DV,
     ACT, DU, DZ, DO, TR,
     lsem, ag_s, ag_r, rs_s, rs_r, nb_s, nb_r, xc_s, xc_r,
@@ -80,13 +80,18 @@
     peers = [sibling, x_peer, y_peer] + z_peer[1:]
     for peer in peers:
         pl.semaphore_signal(barrier, inc=1, device_id=peer, device_id_type=MESH)
+    mine = pl.ds(pl.multiple_of(x * SEQ, SEQ), SEQ)
+    moves = (
+        (norms_hbm, norms), (ain_hbm, ain), (aout_hbm, aout), (fin_hbm, fin), (fout_hbm, fout),
+        (tok_hbm.at[mine], tok), (mem_hbm.at[mine], mem), (cot_hbm.at[mine], cot),
+    )
     fetches = []
-    for number, (src, dst) in enumerate(((tok_hbm, tok), (mem_hbm, mem), (cot_hbm, cot))):
-        fetch = pltpu.make_async_copy(
-            src.at[pl.ds(pl.multiple_of(x * SEQ, SEQ), SEQ)], dst, lsem.at[number]
-        )
+    for number, (src, dst) in enumerate(moves):
+        fetch = pltpu.make_async_copy(src, dst, lsem.at[number])
         fetch.start()
         fetches.append(fetch)
+    for fetch in fetches[:5]:
+        fetch.wait()
 
     NP[...] = jnp.zeros_like(NP)
     NP[0:6, 0:rows_own] = norms[...].astype(BF).astype(F32)
@@ -118,10 +123,13 @@
         flights[key] = pltpu.make_async_remote_copy(
             *whole, *sems, device_id=copies[0][2], device_id_type=MESH
         )
-        pending.append(flights[key])
+        if key[2] == 2:
+            pending.append(flights[key])
 
     def landed(key):
         flights[key].wait_recv()
+        if key[2] < 2:
+            flights[key].wait_send()
 
     def place_of(done, blocks):
         at = {axis: slice(None) if axis in done else me_of[axis] for axis in "xyz"}
@@ -135,7 +143,7 @@
         first, count, route = GATHER[parcel]
         at, where = place_of(route[:phase], pl.ds(first, count))
         part = W.at[where()]
-        sems = (ag_s.at[parcel, phase], ag_r.at[parcel, phase])
+        sems = (ag_s.at[parcel], ag_r.at[parcel, phase])
         if route[phase] == "z":
             at["z"] = pl.ds(0, nz - 1)
         much = W.at[where()]
@@ -187,7 +195,7 @@
 
         at[axis] = pl.ds(0, nz - 1) if axis == "z" else me_of[axis]
         much = G.at[where()]
-        sems = (rs_s.at[parcel, phase], rs_r.at[parcel, phase])
+        sems = (rs_s.at[parcel], rs_r.at[parcel, phase])
         send_all(("sum", parcel, phase), axis, pieces, (much, into if axis == "z" else into.at[0]), sems)
 
     xc = {}
@@ -211,12 +219,11 @@
             XS[number, rows] = make(rows).astype(BF)
             swap_start(number, half)
 
-    def each_rows(body, size=128, start=0, stop=SEQ):
-        def one(step, carry):
-            body(pl.ds(pl.multiple_of(start + step * size, size), size), start + step * size)
-            return carry
-
-        lax.fori_loop(0, (stop - start) // size, one, 0)
+    def each_rows(body, swap=None):
+        for first in range(0, SEQ, 128):
+            if swap is not None and first % 256 == 0:
+                xc[swap, first // 256].wait_recv()
+            body(slice(first, first + 128), first)
 
     def norm_rows(number, rows, values):
         center = values - jnp.mean(values, -1, keepdims=True)
@@ -258,42 +265,35 @@
 
     def attend(number, half):
         count = 256 * (half + 1) if number == 0 else SEQ
-        fill = key_fill(count)
-
-        def body(rows, first):
-            bias = fill
-            if number == 0:
-                row = first + lax.broadcasted_iota(jnp.int32, (128, count), 0)
-                col = lax.broadcasted_iota(jnp.int32, (128, count), 1)
-                bias = jnp.where(col <= row, fill, NEG_FILL)
-            query = Q[number, rows]
-            mixed = jnp.zeros((128, COLS), F32)
-            for head in range(HEADS_HERE):
-                scores = nt(query, KM[number, head, :count]) + bias
-                expo = jnp.exp(scores - jnp.max(scores, -1, keepdims=True))
-                prob = (expo * (1.0 / jnp.sum(expo, -1, keepdims=True))).astype(BF)
-                PR[number, head, rows, :count] = prob
-                mixed = mixed + nn(prob, VM[number, head, :count])
-            A[number, rows] = mixed.astype(BF)
-
-        each_rows(body, start=half * 256, stop=half * 256 + 256)
+        rows = slice(half * 256, half * 256 + 256)
+        bias = key_fill(count)
+        if number == 0:
+            row = half * 256 + lax.broadcasted_iota(jnp.int32, (256, count), 0)
+            col = lax.broadcasted_iota(jnp.int32, (256, count), 1)
+            bias = jnp.where(col <= row, bias, NEG_FILL)
+        query = Q[number, rows]
+        mixed = jnp.zeros((256, COLS), F32)
+        for head in range(HEADS_HERE):
+            scores = nt(query, KM[number, head, :count]) + bias
+            expo = jnp.exp(scores - jnp.max(scores, -1, keepdims=True))
+            prob = (expo * (1.0 / jnp.sum(expo, -1, keepdims=True))).astype(BF)
+            PR[number, head, rows, :count] = prob
+            mixed = mixed + nn(prob, VM[number, head, :count])
+        A[number, rows] = mixed.astype(BF)
 
     def attend_back(number, half):
         count = 256 * (half + 1) if number == 0 else SEQ
-
-        def body(rows, first):
-            grad_o = DO[rows]
-            grad_q = jnp.zeros((128, COLS), F32)
-            for head in range(HEADS_HERE):
-                grad_p = nt(grad_o, VM[number, head, :count])
-                prob = PR[number, head, rows, :count].astype(F32)
-                inner = jnp.sum(prob * grad_p, -1, keepdims=True)
-                grad_s = (prob * (grad_p - inner)).astype(BF)
-                DS[head, rows, :count] = grad_s
-                grad_q = grad_q + nn(grad_s, KM[number, head, :count])
-            DQ[rows] = (grad_q * HD**-0.5).astype(BF)
-
-        each_rows(body, start=half * 256, stop=half * 256 + 256)
+        rows = slice(half * 256, half * 256 + 256)
+        grad_o = DO[rows]
+        grad_q = jnp.zeros((256, COLS), F32)
+        for head in range(HEADS_HERE):
+            grad_p = nt(grad_o, VM[number, head, :count])
+            prob = PR[number, head, rows, :count].astype(F32)
+            inner = jnp.sum(prob * grad_p, -1, keepdims=True)
+            grad_s = (prob * (grad_p - inner)).astype(BF)
+            DS[head, rows, :count] = grad_s
+            grad_q = grad_q + nn(grad_s, KM[number, head, :count])
+        DQ[rows] = (grad_q * HD**-0.5).astype(BF)
 
     def turned_product(number, table, source, target):
         source_t = source[...].T
@@ -331,12 +331,11 @@
         NGR[...] = jnp.zeros_like(NGR)
 
     def fetched():
-        for fetch in fetches:
+        for fetch in fetches[5:]:
             fetch.wait()
 
     def first_norm():
         each_rows(lambda rows, first: norm_rows(0, rows, tok[rows].astype(F32)))
-        HT[0] = H[0].T
 
     def cotangent_rows():
         def dead_rows(rows, first):
@@ -365,10 +364,6 @@
         K[1] = nn(mem[...], weight(WK2)).astype(BF)
         V[1] = nn(mem[...], weight(WV2)).astype(BF)
         split_heads(1)
-
-    def swapped(number):
-        xc[number, 0].wait_recv()
-        xc[number, 1].wait_recv()
 
     def second_norm():
         def second_rows(rows, first):
@@ -376,13 +371,13 @@
             XF[rows] = values
             norm_rows(1, rows, values)
 
-        each_rows(second_rows)
+        each_rows(second_rows, 0)
 
     def cross_queries():
         Q[1] = (nn(H[1], weight(WQ2)) * HD**-0.5).astype(BF)
 
     def turn(number):
-        HT[1 + number] = H[number].T
+        HT[number + 1 if number else 0] = H[number].T
 
     def third_norm():
         def third_rows(rows, first):
@@ -390,7 +385,7 @@
             XF[rows] = values
             norm_rows(2, rows, values)
 
-        each_rows(third_rows)
+        each_rows(third_rows, 1)
 
     def hidden_chunk(chunk):
         up, down = weight(8 + 2 * chunk), weight(9 + 2 * chunk)
@@ -411,7 +406,8 @@
                 OACC[rows] += nt(act, down)
                 DHA[rows] += nt(grad_u, up)
 
-        each_rows(hidden_rows, size=256)
+        for half in range(2):
+            hidden_rows(slice(half * 256, half * 256 + 256), half * 256)
 
     def hidden_grads(chunk):
         put_grad(8 + 2 * chunk, nn(HT[3], DU[...]))
@@ -429,7 +425,7 @@
             DX[rows] = grad
             H[2, rows] = grad.astype(BF)
 
-        each_rows(one)
+        each_rows(one, 3)
 
     def back_second():
         def one(rows, first):
@@ -437,14 +433,14 @@
             DX[rows] = grad
             H[2, rows] = grad.astype(BF)
 
-        each_rows(one)
+        each_rows(one, 4)
 
     def back_first():
         def one(rows, first):
             grad = DX[rows] + norm_back(0, rows, swap_sum(5, rows))
             tgrad[x, rows] = grad.astype(BF)
 
-        each_rows(one)
+        each_rows(one, 5)
 
     def project_back(number):
         block = WO2 if number else WO1
@@ -476,12 +472,13 @@
 
     def share_done(number):
         shares[number, 1].wait_recv()
+        store((bout, tgrad)[number], (bout_hbm, tgrad_hbm)[number])
 
     def out_rows():
         def one(rows, first):
             bout[x, rows] = (XF[rows] + swap_sum(2, rows)).astype(BF)
 
-        each_rows(one)
+        each_rows(one, 2)
 
     norm_sends = {}
 
@@ -513,55 +510,22 @@
         column = pl.ds(pl.multiple_of(dp * rows_own // 128 * 128, 128), 128)
         nsum[...] = pltpu.roll(NT[:, column], lax.rem(128 - lane_at, 128), 1)
 
+    stored = []
+
+    def store(src, dst):
+        copy = pltpu.make_async_copy(src, dst, lsem.at[8 + len(stored)])
+        copy.start()
+        stored.append(copy)
+
     def finish():
+        store(gsum, gsum_hbm)
+        store(nsum, nsum_hbm)
         for copy in pending:
             copy.wait_send()
-
-    plan = (
-        (gather, 0, 0), (gather, 1, 0), (norms_pass,), (gather, 14, 0), (gather, 15, 0),
-        (gather, 2, 0), (gather, 3, 0), (gather, 0, 1), (gather, 1, 1), (gather, 4, 0), (gather, 5, 0),
-        (gains,), (fetched,), (first_norm,),
-        (gather, 2, 1), (gather, 3, 1), (gather, 0, 2), (gather, 1, 2), (gather, 14, 1), (gather, 15, 1),
-        (gather, 6, 0), (gather, 7, 0), (cotangent_rows,), (memory_turned,),
-        (gather, 4, 1), (gather, 5, 1), (gather, 2, 2), (gather, 3, 2), (gather, 8, 0), (gather, 9, 0),
-        (gather, 0, 3), (gather, 1, 3), (self_queries,),
-        (gather, 6, 1), (gather, 7, 1), (gather, 4, 2), (gather, 5, 2), (gather, 10, 0), (gather, 11, 0),
-        (gather, 2, 3), (self_values,), (attend, 0, 0),
-        (gather, 8, 1), (gather, 9, 1), (gather, 6, 2), (gather, 7, 2), (gather, 12, 0), (gather, 13, 0),
-        (attend, 0, 1), (gather, 3, 3), (project, 0),
-        (gather, 10, 1), (gather, 11, 1), (gather, 8, 2), (gather, 9, 2),
-        (gather, 4, 3), (gather, 5, 3), (memory_keys,), (gather, 14, 2), (gather, 15, 2),
-        (swapped, 0), (second_norm,), (gather, 12, 1), (gather, 13, 1), (gather, 10, 2), (gather, 11, 2),
-        (gather, 6, 3), (cross_queries,), (attend, 1, 0), (gather, 12, 2), (gather, 13, 2),
-        (attend, 1, 1), (gather, 7, 3), (project, 1), (turn, 1), (swapped, 1), (third_norm,), (turn, 2),
-        (gather, 8, 3), (gather, 9, 3), (hidden_chunk, 0), (hidden_grads, 0), (total, 0, 0), (total, 1, 0),
-        (gather, 10, 3), (gather, 11, 3), (hidden_chunk, 1), (hidden_grads, 1), (total, 2, 0), (total, 3, 0),
-        (gather, 12, 3), (gather, 13, 3), (hidden_chunk, 2), (hidden_grads, 2), (total, 4, 0), (total, 5, 0),
-        (gather, 14, 3), (gather, 15, 3), (hidden_chunk, 3), (hidden_swap,),
-        (hidden_grads, 3), (total, 6, 0), (total, 7, 0), (out_swap,),
-        (total, 2, 1), (total, 3, 1),
-        (swapped, 3), (back_third,), (project_back, 1), (total, 8, 0),
-        (total, 4, 1), (total, 5, 1), (value_back, 1), (weight_grad, WV2, 1, 2), (total, 9, 0),
-        (total, 0, 1), (total, 1, 1), (attend_back, 1, 0),
-        (total, 6, 1), (total, 7, 1), (total, 2, 2), (total, 3, 2), (attend_back, 1, 1),
-        (cross_query_back,), (weight_grad, WQ2, 2, 0), (total, 10, 0),
-        (total, 4, 2), (total, 5, 2), (total, 8, 1), (total, 0, 2), (total, 1, 2),
-        (key_back, 1), (weight_grad, WK2, 1, 1), (total, 11, 0), (total, 9, 1),
-        (swapped, 2), (out_rows,), (share_start, 0),
-        (swapped, 4), (back_second,), (project_back, 0), (total, 12, 0),
-        (total, 6, 2), (total, 7, 2), (total, 10, 1), (value_back, 0), (weight_grad, WV1, 0, 2), (total, 13, 0),
-        (total, 8, 2), (total, 9, 2), (attend_back, 0, 0), (total, 11, 1), (total, 10, 2),
-        (total, 12, 1), (attend_back, 0, 1), (weight_grad, WQ1, 0, 0), (total, 14, 0),
-        (total, 13, 1), (total, 11, 2),
-        (key_back, 0), (weight_grad, WK1, 0, 1), (total, 15, 0), (self_back,),
-        (total, 12, 2), (share_pass, 0), (total, 0, 3), (total, 1, 3), (total, 2, 3), (total, 3, 3),
-        (swapped, 5), (back_first,), (share_start, 1), (norm_grads_start,), (total, 14, 1), (total, 13, 2),
-        (total, 4, 3), (total, 5, 3), (total, 15, 1), (norm_grads_mid,),
-        (total, 6, 3), (total, 7, 3), (total, 14, 2), (norm_grads_last,),
-        (total, 8, 3), (total, 9, 3), (total, 15, 2), (share_pass, 1),
-        (total, 10, 3), (total, 11, 3), (total, 12, 3), (norm_grads_done,),
-        (total, 13, 3), (total, 14, 3), (total, 15, 3), (share_done, 0), (share_done, 1), (finish,),
-    )
+        for copy in stored:
+            copy.wait()
+
+    plan = ((gather,0,0,),(gather,1,0,),(gather,2,0,),(gather,4,0,),(gather,3,0,),(gather,5,0,),(gather,14,0,),(gather,15,0,),(fetched,),(memory_turned,),(cotangent_rows,),(norms_pass,),(gather,6,0,),(gather,0,1,),(gather,7,0,),(gather,14,1,),(gather,15,1,),(gains,),(gather,1,1,),(gather,8,0,),(first_norm,),(turn,0,),(gather,2,1,),(gather,9,0,),(gather,0,2,),(gather,4,1,),(gather,14,2,),(gather,1,2,),(gather,3,1,),(gather,2,2,),(gather,5,1,),(gather,4,2,),(gather,0,3,),(gather,6,1,),(gather,7,1,),(gather,3,2,),(gather,11,0,),(gather,1,3,),(self_queries,),(gather,8,1,),(gather,10,0,),(gather,6,2,),(gather,2,3,),(self_values,),(attend,0,0,),(gather,9,1,),(gather,13,0,),(gather,3,3,),(gather,5,2,),(gather,12,0,),(attend,0,1,),(gather,15,2,),(gather,4,3,),(gather,8,2,),(gather,14,3,),(project,0,),(gather,7,2,),(gather,11,1,),(gather,5,3,),(memory_keys,),(second_norm,),(gather,6,3,),(cross_queries,),(gather,10,1,),(attend,1,0,),(gather,13,1,),(gather,9,2,),(gather,7,3,),(gather,12,1,),(attend,1,1,),(gather,8,3,),(gather,10,2,),(project,1,),(gather,11,2,),(turn,1,),(gather,9,3,),(gather,13,2,),(third_norm,),(gather,15,3,),(gather,12,2,),(turn,2,),(hidden_chunk,0,),(gather,10,3,),(hidden_grads,0,),(total,0,0,),(gather,11,3,),(hidden_chunk,1,),(hidden_grads,1,),(total,2,0,),(total,3,0,),(total,1,0,),(gather,12,3,),(gather,13,3,),(hidden_chunk,2,),(hidden_grads,2,),(total,4,0,),(total,5,0,),(hidden_chunk,3,),(hidden_swap,),(out_swap,),(hidden_grads,3,),(total,6,0,),(total,3,1,),(total,2,1,),(total,0,1,),(total,7,0,),(back_third,),(out_rows,),(share_start,0,),(project_back,1,),(attend_back,1,0,),(total,8,0,),(total,6,1,),(total,4,1,),(attend_back,1,1,),(total,3,2,),(total,0,2,),(total,5,1,),(value_back,1,),(total,1,1,),(total,2,2,),(weight_grad,WV2,1,2,),(total,9,0,),(total,7,1,),(cross_query_back,),(share_pass,0,),(weight_grad,WQ2,2,0,),(total,10,0,),(key_back,1,),(total,6,2,),(total,4,2,),(total,8,1,),(share_done,0,),(back_second,),(total,5,2,),(project_back,0,),(total,1,2,),(total,9,1,),(total,12,0,),(attend_back,0,0,),(total,7,2,),(value_back,0,),(weight_grad,WV1,0,2,),(total,13,0,),(attend_back,0,1,),(total,8,2,),(total,10,1,),(weight_grad,WK2,1,1,),(total,11,0,),(total,9,2,),(key_back,0,),(self_back,),(weight_grad,WQ1,0,0,),(total,14,0,),(total,12,1,),(total,13,1,),(weight_grad,WK1,0,1,),(total,15,0,),(total,4,3,),(back_first,),(share_start,1,),(total,9,3,),(total,10,2,),(norm_grads_start,),(total,11,1,),(total,2,3,),(total,3,3,),(total,8,3,),(total,6,3,),(total,5,3,),(total,0,3,),(total,7,3,),(total,1,3,),(total,14,1,),(total,12,2,),(total,15,1,),(total,13,2,),(total,11,2,),(total,12,3,),(total,10,3,),(share_pass,1,),(norm_grads_mid,),(total,15,2,),(total,13,3,),(share_done,1,),(norm_grads_last,),(total,14,2,),(total,11,3,),(total,14,3,),(total,15,3,),(norm_grads_done,),(finish,),)
     for step, *of in plan:
         step(*of)
 
@@ -573,27 +537,55 @@
     return moment_new, weight_new, average_new
 
 
-def update_kernel(rate_scale, gsum, nsum, tlow, *refs):
-    weights, moments, averages, outs = refs[0:5], refs[5:10], refs[10:15], refs[15:]
-    tgrad_out, results = outs[0], outs[1:]
-    tgrad_out[...] = tlow[...].astype(F32)
-
-    def one(which, at, grad):
-        found = update(
-            weights[which][at],
-            grad,
-            moments[which][at],
-            averages[which][at],
-            BASE_RATES[which] * rate_scale,
-        )
-        for number, value in enumerate((grad, *found)):
-            results[4 * which + number][at] = value
-
-    for block, (array, index) in enumerate(BLOCK_OF):
-        at = (index,) if array < 2 else (slice(None), slice(index * 128, index * 128 + 128))
-        one(array, at, gsum[block])
-    wide = weights[4].shape[1]
-    one(4, (slice(None), slice(None)), nsum[0:6, 0:wide])
+def update_kernel(rate_scale, gsum_hbm, nsum_hbm, tlow_hbm, bout_hbm, *refs):
+    sources, targets = refs[0:15], refs[15:37]
+    gsum, nsum, tlow, bout, tgrad, *held, in_sems, out_sems = refs[37:]
+    fetched, results = held[0:15], held[15:35]
+    moves = (
+        (tlow_hbm, tlow), (bout_hbm, bout), (gsum_hbm, gsum), (nsum_hbm, nsum),
+        *zip(sources, fetched),
+    )
+    fetches = [
+        pltpu.make_async_copy(src, dst, in_sems.at[number])
+        for number, (src, dst) in enumerate(moves)
+    ]
+    for fetch in fetches:
+        fetch.start()
+    stores = []
+
+    def store(src, number):
+        copy = pltpu.make_async_copy(src, targets[number], out_sems.at[number])
+        copy.start()
+        stores.append(copy)
+
+    fetches[0].wait()
+    tgrad[...] = tlow[...].astype(F32)
+    store(tgrad, 1)
+    fetches[1].wait()
+    store(bout, 0)
+    fetches[2].wait()
+    fetches[3].wait()
+    for which in range(5):
+        weight, moment, average = fetched[which], fetched[5 + which], fetched[10 + which]
+        for turn in range(3):
+            fetches[4 + 5 * turn + which].wait()
+        if which < 4:
+            parts = [
+                ((index,) if which < 2 else (slice(None), slice(index * 128, index * 128 + 128)), gsum[block])
+                for block, (array, index) in enumerate(BLOCK_OF)
+                if array == which
+            ]
+        else:
+            parts = [((slice(None), slice(None)), nsum[0:6, 0 : weight.shape[1]])]
+        for at, grad in parts:
+            rate = BASE_RATES[which] * rate_scale
+            found = update(weight[at], grad, moment[at], average[at], rate)
+            for number, value in enumerate((grad, *found)):
+                results[4 * which + number][at] = value
+        for number in range(4):
+            store(results[4 * which + number], 2 + 4 * which + number)
+    for copy in stores:
+        copy.wait()
 
 
 def per_device(nz, *args):
@@ -601,7 +593,6 @@
     moments, averages = args[10:15], args[15:20]
     own = attn_in.shape[1]
     whole = (nz, 2, own, 128)
-    vmem = pl.BlockSpec(memory_space=pltpu.VMEM)
     smem = pl.BlockSpec(memory_space=pltpu.SMEM)
     hbm = pl.BlockSpec(memory_space=pl.ANY)
     dma = pltpu.SemaphoreType.DMA
@@ -623,6 +614,8 @@
 
     landings = [[landing(parcel, phase) for phase in range(3)] for parcel in SUM]
     scratch = [
+        f32(BLOCKS, own, 128), f32(8, 128), bf(2, SEQ, WIDTH), bf(2, SEQ, WIDTH),
+        *[f32(*array.shape) for array in (attn_in, attn_out, ffn_in, ffn_out, norms)],
         bf(SEQ, WIDTH), bf(SEQ, WIDTH), bf(SEQ, WIDTH),
         bf(2, BLOCKS, *whole), bf(2, BLOCKS, *whole),
         landings,
@@ -639,7 +632,8 @@
         bf(2, SEQ, COLS), f32(SEQ, WIDTH),
         bf(SEQ, COLS), bf(SEQ, COLS), bf(SEQ, COLS),
         bf(SEQ, COLS), bf(SEQ, COLS), bf(SEQ, WIDTH), bf(SEQ, COLS), bf(COLS, SEQ),
-        dma((3,)), *[dma((len(GATHER), 3))] * 2, *[dma((len(SUM), 3))] * 2,
+        dma((12,)), dma((len(GATHER),)), dma((len(GATHER), 3)),
+        dma((len(SUM),)), dma((len(SUM), 3)),
         dma((nz,)), dma((nz,)),
         dma((6, 2)), dma((6, 2)),
         dma((nz + 1,)), dma((nz + 1,)), dma((2, 2)), dma((2, 2)),
@@ -652,8 +646,8 @@
             jax.ShapeDtypeStruct((2, SEQ, WIDTH), BF),
             jax.ShapeDtypeStruct((2, SEQ, WIDTH), BF),
         ),
-        in_specs=[hbm] * 3 + [smem] * 2 + [vmem] * 5,
-        out_specs=(vmem,) * 4,
+        in_specs=[hbm] * 3 + [smem] * 2 + [hbm] * 5,
+        out_specs=(hbm,) * 4,
         scratch_shapes=scratch,
         compiler_params=pltpu.CompilerParams(
             collective_id=0, has_side_effects=True, vmem_limit_bytes=58 * 2**20
@@ -663,11 +657,22 @@
     rate_scale = float(lax.axis_size("dp") * tokens.shape[0]) ** -0.5
     results = pl.pallas_call(
         functools.partial(update_kernel, rate_scale),
-        out_shape=(jax.ShapeDtypeStruct((2, SEQ, WIDTH), F32),)
-        + tuple(jax.ShapeDtypeStruct(w.shape, F32) for w in weights for _ in range(4)),
-        compiler_params=pltpu.CompilerParams(vmem_limit_bytes=32 * 2**20),
-    )(gsum, nsum, tlow, *weights, *moments, *averages)
-    return (bout.reshape(tokens.shape), results[0].reshape(tokens.shape), *results[1:])
+        out_shape=(
+            jax.ShapeDtypeStruct((2, SEQ, WIDTH), BF),
+            jax.ShapeDtypeStruct((2, SEQ, WIDTH), F32),
+            *[jax.ShapeDtypeStruct(w.shape, F32) for w in weights for _ in range(4)],
+        ),
+        in_specs=[hbm] * 19,
+        out_specs=(hbm,) * 22,
+        scratch_shapes=[
+            f32(BLOCKS, own, 128), f32(8, 128), bf(2, SEQ, WIDTH), bf(2, SEQ, WIDTH), f32(2, SEQ, WIDTH),
+            *[f32(*w.shape) for w in (*weights, *moments, *averages)],
+            *[f32(*w.shape) for w in weights for _ in range(4)],
+            dma((19,)), dma((22,)),
+        ],
+        compiler_params=pltpu.CompilerParams(vmem_limit_bytes=63 * 2**20),
+    )(gsum, nsum, tlow, bout, *weights, *moments, *averages)
+    return (results[0].reshape(tokens.shape), results[1].reshape(tokens.shape), *results[2:])
 
 
 def solution(mesh):

time: 113 us -> 102 us (0.903)
  Pallas kernels: 108 us -> 101 us
  local copies, waits for them, and re-layouts: 3.97 us -> 0 us
    pallas_call x1, Pallas kernels: 106 us -> 96.5 us  [per_device(): pl.pallas_call(functools.partial(layer_kernel, nz), out_shape=(jax.ShapeD...]
    unnamed x39 -> x0, local copies, waits for them, and re-layouts: 3.97 us -> none
    pallas_call x1, Pallas kernels: 2.24 us -> 4.12 us  [per_device(): pl.pallas_call(functools.partial(update_kernel, rate_scale), out_shape=(j...]
where the time goes in v3:
time: 102 us; the launch traced here: 101 us
  Pallas kernels  101 us (99%)
    pallas_call x1, Pallas kernels, per_device(): pl.pallas_call(functools.partial(layer_kernel, nz), out_shape=(jax.ShapeD...  96.5 us
    pallas_call x1, Pallas kernels, per_device(): pl.pallas_call(functools.partial(update_kernel, rate_scale), out_shape=(j...  4.12 us

profile of v3, /device:TPU:0, one launch (start us, length us, event | category | flops | bytes accessed | tf_op | source)
XLA Modules:
  0.0 101.4 jit_solution(13443973819708613431)
XLA Ops:
  0.7 96.5 %shard_map.363 = (f32[16,64,128]{2,1,0:T(8,128)}, f32[8,128]{1,0:T(8,128)}, bf16[2,512,512]{2,1,0:T(8,128)(2,1)}, bf16[2,512,512]{2,1,0:T(8,128)(2,1)}) custom-call(bf16[1024,512]{1,0:T(8,128)(2,1)} %tok_hbm.1, bf16[1024,512]{1,0:T(8,128)(2,1)} %mem_hbm.1, bf16[1024,512]{1,0:T(8,128)(2,1)} %cot_hbm.1, s32[2]{0:T(128)} %len_ref.1, s32[2]{0:T(128)} %brk_ref.1, ...), custom_call_target="tpu_custom_call" | custom-call | tf_op jit(solution)/shard_map/pallas_call | solution.py:641
  97.1 4.1 %shard_map.364 = (bf16[2,512,512]{2,1,0:T(8,128)(2,1)}, f32[2,512,512]{2,1,0:T(8,128)}, f32[6,64,128]{2,1,0:T(8,128)}, f32[6,64,128]{2,1,0:T(8,128)}, f32[6,64,1...) custom-call(f32[16,64,128]{2,1,0:T(8,128)} %get-tuple-element.48.gsu, ...), custom_call_target="tpu_custom_call" | custom-call | tf_op jit(solution)/shard_map/pallas_call | solution.py:658

commit v4 on v3

--- a/solution.py
+++ b/solution.py
@@ -32,10 +32,10 @@
 WQ1, WK1, WV1, WO1, WK2, WV2, WQ2, WO2 = range(8)
 GATHER = tuple((block, 1, ("zyx", "zxy")[block % 2]) for block in range(14)) + ((14, 1, "xyz"), (15, 1, "yxz"))
 SUM = (
-    (8, 1, "zxy"), (9, 1, "zxy"), (10, 1, "yzx"), (11, 1, "xyz"),
-    (12, 1, "yxz"), (13, 1, "yxz"), (14, 1, "xzy"), (15, 1, "yxz"),
-    (7, 1, "yzx"), (5, 1, "yxz"), (6, 1, "xyz"), (4, 1, "xyz"),
-    (3, 1, "xzy"), (2, 1, "yzx"), (0, 1, "yzx"), (1, 1, "yxz"),
+    (8, 1, "xyz"), (9, 1, "zxy"), (10, 1, "yxz"), (11, 1, "xyz"),
+    (12, 1, "xyz"), (13, 1, "xyz"), (14, 1, "yzx"), (15, 1, "zyx"),
+    (7, 1, "zxy"), (5, 1, "xyz"), (6, 1, "yxz"), (4, 1, "yzx"),
+    (3, 1, "yxz"), (2, 1, "yzx"), (0, 1, "xyz"), (1, 1, "xyz"),
 )
 
 
@@ -525,7 +525,41 @@
         for copy in stored:
             copy.wait()
 
-    plan = ((gather,0,0,),(gather,1,0,),(gather,2,0,),(gather,4,0,),(gather,3,0,),(gather,5,0,),(gather,14,0,),(gather,15,0,),(fetched,),(memory_turned,),(cotangent_rows,),(norms_pass,),(gather,6,0,),(gather,0,1,),(gather,7,0,),(gather,14,1,),(gather,15,1,),(gains,),(gather,1,1,),(gather,8,0,),(first_norm,),(turn,0,),(gather,2,1,),(gather,9,0,),(gather,0,2,),(gather,4,1,),(gather,14,2,),(gather,1,2,),(gather,3,1,),(gather,2,2,),(gather,5,1,),(gather,4,2,),(gather,0,3,),(gather,6,1,),(gather,7,1,),(gather,3,2,),(gather,11,0,),(gather,1,3,),(self_queries,),(gather,8,1,),(gather,10,0,),(gather,6,2,),(gather,2,3,),(self_values,),(attend,0,0,),(gather,9,1,),(gather,13,0,),(gather,3,3,),(gather,5,2,),(gather,12,0,),(attend,0,1,),(gather,15,2,),(gather,4,3,),(gather,8,2,),(gather,14,3,),(project,0,),(gather,7,2,),(gather,11,1,),(gather,5,3,),(memory_keys,),(second_norm,),(gather,6,3,),(cross_queries,),(gather,10,1,),(attend,1,0,),(gather,13,1,),(gather,9,2,),(gather,7,3,),(gather,12,1,),(attend,1,1,),(gather,8,3,),(gather,10,2,),(project,1,),(gather,11,2,),(turn,1,),(gather,9,3,),(gather,13,2,),(third_norm,),(gather,15,3,),(gather,12,2,),(turn,2,),(hidden_chunk,0,),(gather,10,3,),(hidden_grads,0,),(total,0,0,),(gather,11,3,),(hidden_chunk,1,),(hidden_grads,1,),(total,2,0,),(total,3,0,),(total,1,0,),(gather,12,3,),(gather,13,3,),(hidden_chunk,2,),(hidden_grads,2,),(total,4,0,),(total,5,0,),(hidden_chunk,3,),(hidden_swap,),(out_swap,),(hidden_grads,3,),(total,6,0,),(total,3,1,),(total,2,1,),(total,0,1,),(total,7,0,),(back_third,),(out_rows,),(share_start,0,),(project_back,1,),(attend_back,1,0,),(total,8,0,),(total,6,1,),(total,4,1,),(attend_back,1,1,),(total,3,2,),(total,0,2,),(total,5,1,),(value_back,1,),(total,1,1,),(total,2,2,),(weight_grad,WV2,1,2,),(total,9,0,),(total,7,1,),(cross_query_back,),(share_pass,0,),(weight_grad,WQ2,2,0,),(total,10,0,),(key_back,1,),(total,6,2,),(total,4,2,),(total,8,1,),(share_done,0,),(back_second,),(total,5,2,),(project_back,0,),(total,1,2,),(total,9,1,),(total,12,0,),(attend_back,0,0,),(total,7,2,),(value_back,0,),(weight_grad,WV1,0,2,),(total,13,0,),(attend_back,0,1,),(total,8,2,),(total,10,1,),(weight_grad,WK2,1,1,),(total,11,0,),(total,9,2,),(key_back,0,),(self_back,),(weight_grad,WQ1,0,0,),(total,14,0,),(total,12,1,),(total,13,1,),(weight_grad,WK1,0,1,),(total,15,0,),(total,4,3,),(back_first,),(share_start,1,),(total,9,3,),(total,10,2,),(norm_grads_start,),(total,11,1,),(total,2,3,),(total,3,3,),(total,8,3,),(total,6,3,),(total,5,3,),(total,0,3,),(total,7,3,),(total,1,3,),(total,14,1,),(total,12,2,),(total,15,1,),(total,13,2,),(total,11,2,),(total,12,3,),(total,10,3,),(share_pass,1,),(norm_grads_mid,),(total,15,2,),(total,13,3,),(share_done,1,),(norm_grads_last,),(total,14,2,),(total,11,3,),(total,14,3,),(total,15,3,),(norm_grads_done,),(finish,),)
+    plan = (
+        (gather, 1, 0), (gather, 14, 0), (gather, 0, 0), (gather, 15, 0), (gather, 2, 0), (fetched,),
+        (cotangent_rows,), (gather, 5, 0), (memory_turned,), (gather, 3, 0), (gather, 4, 0), (gather, 14, 1),
+        (norms_pass,), (gather, 15, 1), (gather, 1, 1), (gather, 6, 0), (gather, 0, 1), (gather, 7, 0),
+        (gather, 2, 1), (gather, 8, 0), (gains,), (first_norm,), (gather, 5, 1), (turn, 0), (gather, 10, 0),
+        (gather, 1, 2), (gather, 3, 1), (gather, 9, 0), (gather, 0, 2), (gather, 4, 1), (gather, 11, 0),
+        (gather, 2, 2), (gather, 6, 1), (gather, 13, 0), (gather, 5, 2), (gather, 7, 1), (gather, 12, 0),
+        (gather, 3, 2), (gather, 14, 2), (gather, 1, 3), (gather, 0, 3), (self_queries,), (gather, 8, 1),
+        (gather, 4, 2), (gather, 9, 1), (gather, 10, 1), (gather, 6, 2), (gather, 2, 3), (self_values,),
+        (attend, 0, 0), (gather, 15, 2), (gather, 5, 3), (attend, 0, 1), (gather, 11, 1), (gather, 7, 2),
+        (gather, 12, 1), (gather, 13, 1), (gather, 3, 3), (project, 0), (gather, 4, 3), (memory_keys,),
+        (gather, 8, 2), (second_norm,), (gather, 9, 2), (turn, 1), (gather, 14, 3), (gather, 10, 2),
+        (gather, 6, 3), (cross_queries,), (attend, 1, 1), (gather, 7, 3), (gather, 11, 2), (attend, 1, 0),
+        (gather, 13, 2), (gather, 12, 2), (project, 1), (gather, 15, 3), (gather, 9, 3), (gather, 8, 3),
+        (third_norm,), (hidden_chunk, 0), (turn, 2), (hidden_grads, 0), (total, 0, 0), (total, 1, 0),
+        (gather, 10, 3), (gather, 11, 3), (hidden_chunk, 1), (hidden_grads, 1), (total, 3, 0), (total, 2, 0),
+        (gather, 13, 3), (gather, 12, 3), (hidden_chunk, 2), (hidden_grads, 2), (total, 4, 0),
+        (hidden_chunk, 3), (out_swap,), (hidden_swap,), (total, 0, 1), (hidden_grads, 3), (total, 6, 0),
+        (total, 7, 0), (total, 5, 0), (out_rows,), (share_start, 0), (back_third,), (project_back, 1),
+        (attend_back, 1, 0), (total, 3, 1), (value_back, 1), (total, 4, 1), (total, 8, 0),
+        (attend_back, 1, 1), (weight_grad, WQ2, 2, 0), (total, 10, 0), (cross_query_back,),
+        (weight_grad, WV2, 1, 2), (key_back, 1), (total, 9, 0), (total, 5, 1), (back_second,),
+        (project_back, 0), (attend_back, 0, 0), (total, 6, 1), (total, 7, 1), (total, 1, 1), (total, 2, 1),
+        (total, 12, 0), (attend_back, 0, 1), (total, 10, 1), (total, 4, 2), (share_pass, 0), (total, 0, 2),
+        (weight_grad, WQ1, 0, 0), (total, 14, 0), (weight_grad, WK2, 1, 1), (total, 11, 0), (key_back, 0),
+        (total, 3, 2), (weight_grad, WK1, 0, 1), (share_done, 0), (value_back, 0), (total, 9, 1),
+        (total, 8, 1), (total, 15, 0), (total, 2, 2), (total, 1, 2), (total, 5, 2), (weight_grad, WV1, 0, 2),
+        (total, 13, 0), (self_back,), (total, 10, 2), (total, 12, 1), (total, 4, 3), (total, 0, 3),
+        (back_first,), (total, 11, 1), (total, 14, 1), (norm_grads_start,), (share_start, 1), (total, 8, 2),
+        (total, 3, 3), (total, 1, 3), (total, 2, 3), (total, 9, 2), (total, 5, 3), (total, 15, 1),
+        (total, 13, 1), (total, 10, 3), (norm_grads_mid,), (total, 6, 2), (total, 7, 2), (total, 8, 3),
+        (total, 12, 2), (total, 11, 2), (total, 14, 2), (total, 9, 3), (norm_grads_last,), (total, 15, 2),
+        (share_pass, 1), (total, 6, 3), (total, 7, 3), (total, 13, 2), (total, 11, 3), (share_done, 1),
+        (total, 12, 3), (total, 14, 3), (norm_grads_done,), (total, 15, 3), (total, 13, 3), (finish,),
+    )
     for step, *of in plan:
         step(*of)
 

time: 102 us -> 93.1 us (0.913)
  Pallas kernels: 101 us -> 92.1 us
    pallas_call x1, Pallas kernels: 96.5 us -> 88 us  [per_device(): pl.pallas_call(functools.partial(layer_kernel, nz), out_shape=(jax.ShapeD...]
where the time goes in v4:
time: 93.1 us; the launch traced here: 92.9 us
  Pallas kernels  92.1 us (99%)
    pallas_call x1, Pallas kernels, per_device(): pl.pallas_call(functools.partial(layer_kernel, nz), out_shape=(jax.ShapeD...  88 us
    pallas_call x1, Pallas kernels, per_device(): pl.pallas_call(functools.partial(update_kernel, rate_scale), out_shape=(j...  4.12 us

profile of v4, /device:TPU:0, one launch (start us, length us, event | category | flops | bytes accessed | tf_op | source)
XLA Modules:
  0.0 92.9 jit_solution(14036013631542470012)
XLA Ops:
  0.7 88.0 %shard_map.363 = (f32[16,64,128]{2,1,0:T(8,128)}, f32[8,128]{1,0:T(8,128)}, bf16[2,512,512]{2,1,0:T(8,128)(2,1)}, bf16[2,512,512]{2,1,0:T(8,128)(2,1)}) custom-call(bf16[1024,512]{1,0:T(8,128)(2,1)} %tok_hbm.1, bf16[1024,512]{1,0:T(8,128)(2,1)} %mem_hbm.1, bf16[1024,512]{1,0:T(8,128)(2,1)} %cot_hbm.1, s32[2]{0:T(128)} %len_ref.1, s32[2]{0:T(128)} %brk_ref.1, ...), custom_call_target="tpu_custom_call" | custom-call | tf_op jit(solution)/shard_map/pallas_call | solution.py:675
  88.7 4.1 %shard_map.364 = (bf16[2,512,512]{2,1,0:T(8,128)(2,1)}, f32[2,512,512]{2,1,0:T(8,128)}, f32[6,64,128]{2,1,0:T(8,128)}, f32[6,64,128]{2,1,0:T(8,128)}, f32[6,64,1...) custom-call(f32[16,64,128]{2,1,0:T(8,128)} %get-tuple-element.48.gsu, ...), custom_call_target="tpu_custom_call" | custom-call | tf_op jit(solution)/shard_map/pallas_call | solution.py:692

commit v5 on v3

--- a/solution.py
+++ b/solution.py
@@ -30,12 +30,17 @@
     (2, 2), (3, 2), (2, 3), (3, 3),
 )
 WQ1, WK1, WV1, WO1, WK2, WV2, WQ2, WO2 = range(8)
-GATHER = tuple((block, 1, ("zyx", "zxy")[block % 2]) for block in range(14)) + ((14, 1, "xyz"), (15, 1, "yxz"))
+GATHER = (
+    (0, 1, "zyx"), (1, 1, "zxy"), (2, 1, "zyx"), (3, 1, "yxz"),
+    (4, 1, "zyx"), (5, 1, "zxy"), (6, 1, "zyx"), (7, 1, "yxz"),
+    (8, 1, "zyx"), (9, 1, "zxy"), (10, 1, "zyx"), (11, 1, "zxy"),
+    (12, 1, "xyz"), (13, 1, "zyx"), (14, 1, "xyz"), (15, 1, "xyz"),
+)
 SUM = (
-    (8, 1, "zxy"), (9, 1, "zxy"), (10, 1, "yzx"), (11, 1, "xyz"),
-    (12, 1, "yxz"), (13, 1, "yxz"), (14, 1, "xzy"), (15, 1, "yxz"),
-    (7, 1, "yzx"), (5, 1, "yxz"), (6, 1, "xyz"), (4, 1, "xyz"),
-    (3, 1, "xzy"), (2, 1, "yzx"), (0, 1, "yzx"), (1, 1, "yxz"),
+    (8, 1, "xzy"), (9, 1, "zyx"), (10, 1, "xyz"), (11, 1, "yxz"),
+    (12, 1, "yxz"), (13, 1, "yzx"), (14, 1, "yxz"), (15, 1, "zyx"),
+    (7, 1, "zyx"), (5, 1, "yzx"), (6, 1, "yxz"), (4, 1, "xyz"),
+    (3, 1, "yxz"), (2, 1, "yxz"), (0, 1, "xyz"), (1, 1, "yxz"),
 )
 
 
@@ -45,6 +50,11 @@
 
 def nt(left, right):
     return lax.dot_general(left, right, (((1,), (1,)), ((), ())), preferred_element_type=F32)
+
+
+class Flight:
+    def __init__(self, wait_recv, wait_send, relay):
+        self.wait_recv, self.wait_send, self.relay = wait_recv, wait_send, relay
 
 
 def layer_kernel(
@@ -54,7 +64,7 @@
     gsum, nsum, bout, tgrad, ain, aout, fin, fout, norms, tok, mem, cot, W, G, R, NB, NP, GAIN, NGR, NX, NY, NZB, NT,
     XS, XR, XF, XH, IV, OACC, DHA, H, HT, Q, K, V, KM, VM, PR, DS, A, DX, DQ, DK, DV,
     ACT, DU, DZ, DO, TR,
-    lsem, ag_s, ag_r, rs_s, rs_r, nb_s, nb_r, xc_s, xc_r,
+    lsem, ag_s, ag_r, ag_f, rs_s, rs_r, nb_s, nb_r, xc_s, xc_r,
     ng_s, ng_r, out_s, out_r,
 ):
     dp, tensor = lax.axis_index("dp"), lax.axis_index("tensor")
@@ -135,6 +145,53 @@
         at = {axis: slice(None) if axis in done else me_of[axis] for axis in "xyz"}
         return at, lambda: (at["x"], blocks, at["z"], at["y"])
 
+    far = lax.rem(z + 2, nz)
+    in_middle = (z == 1) | (z == 2)
+
+    def z_gather(parcel, part, at, where):
+        sems = (ag_s.at[parcel], ag_r.at[parcel, GATHER[parcel][2].index("z")])
+
+        def copy_to(src, place, send_sem, recv_sem):
+            return pltpu.make_async_remote_copy(
+                src, src, send_sem, recv_sem, device_id=(place * 2 + y, tensor), device_id_type=MESH
+            )
+
+        def of(count):
+            at["z"] = pl.ds(0, count)
+            return W.at[where()]
+
+        copy_to(part, z_of[2], sems[0], ag_f.at[parcel]).start()
+        for s, end in ((1, 3), (3, 0)):
+
+            @pl.when(z != end)
+            def _(s=s):
+                copy_to(part, z_of[s], *sems).start()
+
+        at["z"] = far
+        on = copy_to(W.at[where()], 3 - far, *sems)
+
+        def relay():
+            copy_to(of(1), z_of[2], sems[0], ag_f.at[parcel]).wait_recv()
+
+            @pl.when(in_middle)
+            def _():
+                copy_to(of(3), z_of[2], *sems).wait_send()
+                on.start()
+
+        def wait_recv():
+            copy_to(of(2), z_of[2], *sems).wait_recv()
+
+        def wait_send():
+            @pl.when(in_middle)
+            def _():
+                on.wait_send()
+
+            @pl.when(jnp.logical_not(in_middle))
+            def _():
+                copy_to(of(2), z_of[2], *sems).wait_send()
+
+        return Flight(wait_recv, wait_send, relay)
+
     def gather(parcel, phase):
         if phase > 0:
             landed(("gather", parcel, phase - 1))
@@ -144,12 +201,20 @@
         at, where = place_of(route[:phase], pl.ds(first, count))
         part = W.at[where()]
         sems = (ag_s.at[parcel], ag_r.at[parcel, phase])
+        key = ("gather", parcel, phase)
+        if route[phase] == "z" and nz == 4:
+            flights[key] = z_gather(parcel, part, at, where)
+            if phase == 2:
+                pending.append(flights[key])
+            return
         if route[phase] == "z":
             at["z"] = pl.ds(0, nz - 1)
         much = W.at[where()]
-        send_all(
-            ("gather", parcel, phase), route[phase], lambda place, slot: (part, part), (much, much), sems
-        )
+        send_all(key, route[phase], lambda place, slot: (part, part), (much, much), sems)
+
+    def relay(parcel):
+        if nz == 4:
+            flights["gather", parcel, GATHER[parcel][2].index("z")].relay()
 
     nb_first = [
         send(NB.at[z, y], NB.at[z, y], nb_s.at[s - 1], nb_r.at[s - 1], z_peer[s])
@@ -525,7 +590,44 @@
         for copy in stored:
             copy.wait()
 
-    plan = ((gather,0,0,),(gather,1,0,),(gather,2,0,),(gather,4,0,),(gather,3,0,),(gather,5,0,),(gather,14,0,),(gather,15,0,),(fetched,),(memory_turned,),(cotangent_rows,),(norms_pass,),(gather,6,0,),(gather,0,1,),(gather,7,0,),(gather,14,1,),(gather,15,1,),(gains,),(gather,1,1,),(gather,8,0,),(first_norm,),(turn,0,),(gather,2,1,),(gather,9,0,),(gather,0,2,),(gather,4,1,),(gather,14,2,),(gather,1,2,),(gather,3,1,),(gather,2,2,),(gather,5,1,),(gather,4,2,),(gather,0,3,),(gather,6,1,),(gather,7,1,),(gather,3,2,),(gather,11,0,),(gather,1,3,),(self_queries,),(gather,8,1,),(gather,10,0,),(gather,6,2,),(gather,2,3,),(self_values,),(attend,0,0,),(gather,9,1,),(gather,13,0,),(gather,3,3,),(gather,5,2,),(gather,12,0,),(attend,0,1,),(gather,15,2,),(gather,4,3,),(gather,8,2,),(gather,14,3,),(project,0,),(gather,7,2,),(gather,11,1,),(gather,5,3,),(memory_keys,),(second_norm,),(gather,6,3,),(cross_queries,),(gather,10,1,),(attend,1,0,),(gather,13,1,),(gather,9,2,),(gather,7,3,),(gather,12,1,),(attend,1,1,),(gather,8,3,),(gather,10,2,),(project,1,),(gather,11,2,),(turn,1,),(gather,9,3,),(gather,13,2,),(third_norm,),(gather,15,3,),(gather,12,2,),(turn,2,),(hidden_chunk,0,),(gather,10,3,),(hidden_grads,0,),(total,0,0,),(gather,11,3,),(hidden_chunk,1,),(hidden_grads,1,),(total,2,0,),(total,3,0,),(total,1,0,),(gather,12,3,),(gather,13,3,),(hidden_chunk,2,),(hidden_grads,2,),(total,4,0,),(total,5,0,),(hidden_chunk,3,),(hidden_swap,),(out_swap,),(hidden_grads,3,),(total,6,0,),(total,3,1,),(total,2,1,),(total,0,1,),(total,7,0,),(back_third,),(out_rows,),(share_start,0,),(project_back,1,),(attend_back,1,0,),(total,8,0,),(total,6,1,),(total,4,1,),(attend_back,1,1,),(total,3,2,),(total,0,2,),(total,5,1,),(value_back,1,),(total,1,1,),(total,2,2,),(weight_grad,WV2,1,2,),(total,9,0,),(total,7,1,),(cross_query_back,),(share_pass,0,),(weight_grad,WQ2,2,0,),(total,10,0,),(key_back,1,),(total,6,2,),(total,4,2,),(total,8,1,),(share_done,0,),(back_second,),(total,5,2,),(project_back,0,),(total,1,2,),(total,9,1,),(total,12,0,),(attend_back,0,0,),(total,7,2,),(value_back,0,),(weight_grad,WV1,0,2,),(total,13,0,),(attend_back,0,1,),(total,8,2,),(total,10,1,),(weight_grad,WK2,1,1,),(total,11,0,),(total,9,2,),(key_back,0,),(self_back,),(weight_grad,WQ1,0,0,),(total,14,0,),(total,12,1,),(total,13,1,),(weight_grad,WK1,0,1,),(total,15,0,),(total,4,3,),(back_first,),(share_start,1,),(total,9,3,),(total,10,2,),(norm_grads_start,),(total,11,1,),(total,2,3,),(total,3,3,),(total,8,3,),(total,6,3,),(total,5,3,),(total,0,3,),(total,7,3,),(total,1,3,),(total,14,1,),(total,12,2,),(total,15,1,),(total,13,2,),(total,11,2,),(total,12,3,),(total,10,3,),(share_pass,1,),(norm_grads_mid,),(total,15,2,),(total,13,3,),(share_done,1,),(norm_grads_last,),(total,14,2,),(total,11,3,),(total,14,3,),(total,15,3,),(norm_grads_done,),(finish,),)
+    plan = (
+        (gather, 2, 0), (gather, 1, 0), (gather, 5, 0), (gather, 15, 0), (gather, 3, 0), (gather, 0, 0),
+        (gather, 7, 0), (gather, 12, 0), (gather, 14, 0), (fetched,), (gather, 9, 0), (cotangent_rows,),
+        (gather, 4, 0), (gather, 6, 0), (norms_pass,), (relay, 2), (memory_turned,), (gather, 15, 1),
+        (gather, 3, 1), (relay, 1), (gather, 7, 1), (gather, 12, 1), (gather, 8, 0), (relay, 5),
+        (gather, 14, 1), (gather, 13, 0), (relay, 0), (gains,), (relay, 9), (first_norm,), (relay, 4),
+        (gather, 15, 2), (turn, 0), (relay, 6), (gather, 2, 1), (gather, 1, 1), (relay, 8), (gather, 5, 1),
+        (relay, 13), (gather, 0, 1), (gather, 9, 1), (gather, 11, 0), (gather, 4, 1), (gather, 10, 0),
+        (gather, 2, 2), (gather, 1, 2), (gather, 3, 2), (relay, 15), (gather, 0, 2), (gather, 6, 1),
+        (relay, 11), (gather, 8, 1), (relay, 10), (gather, 4, 2), (gather, 7, 2), (gather, 13, 1),
+        (gather, 2, 3), (gather, 1, 3), (gather, 5, 2), (relay, 3), (gather, 6, 2), (gather, 15, 3),
+        (gather, 0, 3), (self_queries,), (self_values,), (attend, 0, 1), (gather, 11, 1), (gather, 10, 1),
+        (gather, 12, 2), (attend, 0, 0), (gather, 4, 3), (gather, 9, 2), (gather, 8, 2), (relay, 7),
+        (gather, 3, 3), (project, 0), (gather, 5, 3), (memory_keys,), (gather, 6, 3), (gather, 14, 2),
+        (gather, 13, 2), (second_norm,), (cross_queries,), (attend, 1, 1), (relay, 12), (gather, 7, 3),
+        (gather, 11, 2), (gather, 9, 3), (gather, 10, 2), (attend, 1, 0), (gather, 8, 3), (project, 1),
+        (turn, 1), (relay, 14), (gather, 13, 3), (third_norm,), (gather, 12, 3), (hidden_chunk, 0),
+        (gather, 11, 3), (turn, 2), (hidden_grads, 0), (total, 1, 0), (gather, 10, 3), (total, 0, 0),
+        (hidden_chunk, 1), (gather, 14, 3), (hidden_grads, 1), (total, 2, 0), (total, 3, 0),
+        (hidden_chunk, 2), (hidden_grads, 2), (total, 4, 0), (hidden_chunk, 3), (out_swap,), (hidden_swap,),
+        (total, 0, 1), (hidden_grads, 3), (total, 6, 0), (out_rows,), (share_start, 0), (back_third,),
+        (total, 7, 0), (project_back, 1), (attend_back, 1, 0), (total, 5, 0), (attend_back, 1, 1),
+        (weight_grad, WQ2, 2, 0), (total, 3, 1), (total, 10, 0), (cross_query_back,), (value_back, 1),
+        (total, 8, 0), (total, 4, 1), (back_second,), (weight_grad, WV2, 1, 2), (total, 6, 1), (total, 9, 0),
+        (key_back, 1), (share_pass, 0), (weight_grad, WK2, 1, 1), (total, 11, 0), (project_back, 0),
+        (value_back, 0), (total, 12, 0), (weight_grad, WV1, 0, 2), (attend_back, 0, 0), (share_done, 0),
+        (total, 3, 2), (total, 10, 1), (attend_back, 0, 1), (total, 13, 0), (total, 4, 2),
+        (weight_grad, WQ1, 0, 0), (total, 14, 0), (total, 6, 2), (key_back, 0), (self_back,), (total, 7, 1),
+        (total, 5, 1), (total, 12, 1), (total, 2, 1), (weight_grad, WK1, 0, 1), (total, 3, 3), (back_first,),
+        (total, 15, 0), (share_start, 1), (total, 4, 3), (total, 10, 2), (norm_grads_start,), (total, 6, 3),
+        (total, 9, 1), (total, 0, 2), (total, 11, 1), (total, 14, 1), (total, 12, 2), (total, 7, 2),
+        (total, 5, 2), (total, 10, 3), (total, 13, 1), (total, 8, 1), (total, 2, 2), (total, 1, 1),
+        (total, 0, 3), (total, 15, 1), (total, 11, 2), (total, 9, 2), (share_pass, 1), (norm_grads_mid,),
+        (total, 7, 3), (total, 5, 3), (total, 14, 2), (total, 12, 3), (total, 8, 2), (total, 13, 2),
+        (share_done, 1), (total, 1, 2), (total, 2, 3), (norm_grads_last,), (total, 15, 2), (total, 9, 3),
+        (total, 11, 3), (total, 8, 3), (total, 14, 3), (total, 1, 3), (total, 13, 3), (norm_grads_done,),
+        (total, 15, 3), (finish,),
+    )
     for step, *of in plan:
         step(*of)
 
@@ -633,6 +735,7 @@
         bf(SEQ, COLS), bf(SEQ, COLS), bf(SEQ, COLS),
         bf(SEQ, COLS), bf(SEQ, COLS), bf(SEQ, WIDTH), bf(SEQ, COLS), bf(COLS, SEQ),
         dma((12,)), dma((len(GATHER),)), dma((len(GATHER), 3)),
+        dma((len(GATHER),)),
         dma((len(SUM),)), dma((len(SUM), 3)),
         dma((nz,)), dma((nz,)),
         dma((6, 2)), dma((6, 2)),

time: 102 us -> 93.1 us (0.913)
  Pallas kernels: 101 us -> 92.1 us
    pallas_call x1, Pallas kernels: 96.5 us -> 87.9 us  [per_device(): pl.pallas_call(functools.partial(layer_kernel, nz), out_shape=(jax.ShapeD...]
where the time goes in v5:
time: 93.1 us; the launch traced here: 92.9 us
  Pallas kernels  92.1 us (99%)
    pallas_call x1, Pallas kernels, per_device(): pl.pallas_call(functools.partial(layer_kernel, nz), out_shape=(jax.ShapeD...  87.9 us
    pallas_call x1, Pallas kernels, per_device(): pl.pallas_call(functools.partial(update_kernel, rate_scale), out_shape=(j...  4.12 us

profile of v5, /device:TPU:0, one launch (start us, length us, event | category | flops | bytes accessed | tf_op | source)
XLA Modules:
  0.0 92.9 jit_solution(352102315371640091)
XLA Ops:
  0.7 87.9 %shard_map.363 = (f32[16,64,128]{2,1,0:T(8,128)}, f32[8,128]{1,0:T(8,128)}, bf16[2,512,512]{2,1,0:T(8,128)(2,1)}, bf16[2,512,512]{2,1,0:T(8,128)(2,1)}) custom-call(bf16[1024,512]{1,0:T(8,128)(2,1)} %tok_hbm.1, bf16[1024,512]{1,0:T(8,128)(2,1)} %mem_hbm.1, bf16[1024,512]{1,0:T(8,128)(2,1)} %cot_hbm.1, s32[2]{0:T(128)} %len_ref.1, s32[2]{0:T(128)} %brk_ref.1, ...), custom_call_target="tpu_custom_call" | custom-call | tf_op jit(solution)/shard_map/pallas_call | solution.py:744
  88.6 4.1 %shard_map.364 = (bf16[2,512,512]{2,1,0:T(8,128)(2,1)}, f32[2,512,512]{2,1,0:T(8,128)}, f32[6,64,128]{2,1,0:T(8,128)}, f32[6,64,128]{2,1,0:T(8,128)}, f32[6,64,1...) custom-call(f32[16,64,128]{2,1,0:T(8,128)} %get-tuple-element.48.gsu, ...), custom_call_target="tpu_custom_call" | custom-call | tf_op jit(solution)/shard_map/pallas_call | solution.py:761
